TPU v7x, 256 devices: a whole 4x4x8 slice. The times are simulated.
256 devices in a mesh: hst: 32 (over y, x, core), tensor: 8 (over z).
Axes of the slice: x: 4, y: 4, z: 8, core: 2. Of those that a mesh axis runs over, the one named last changes fastest.
Arguments:
- queries: bfloat16 [16384, 8192], P('hst', 'tensor'), may hold values from -220 to 220
- own_kv: bfloat16 [16384, 2048], P('hst', 'tensor'), may hold values from -6 to 6
- retain: int32 [2048, 8], P('hst', 'tensor'), may hold values from 0 to 511, as said below
- anchor_hidden: bfloat16 [1024, 8192], P(('hst', 'tensor')), may hold values from -6 to 6
- w_kv: bfloat16 [8192, 2048], P(None, 'tensor'), may hold values from -0.0625 to 0.0625
Outputs:
- attended: bfloat16 [16384, 8192], P('hst', 'tensor')
Inputs may be any that keep to these rules, and one draw needn't show every extreme that they name: `retain`: each host block and key-value head names 64 distinct local rows, 0 and 511 among them.
All inputs are finite; a program needn't handle non-finite values.
Results may differ from a plain program's by a relative error of at most 0.023.
Values may be sent and summed in bfloat16 or wider, within the bound.
No kernel may reach another device: no remote copies, remote signals or barrier semaphores. Data moves between devices by JAX's collectives and lax.ppermute only.
A program may use at most 128 MiB of HBM per device.

v0:
```python
import jax
import jax.numpy as jnp
from jax import lax
from jax.sharding import PartitionSpec as P

H = 64
KVH = 8
HD = 128


def attend(carry, query_local, keys, mask_fn):
    count = keys.shape[0]
    width = min(count, 512)
    steps = count // width
    scale = 1.0 / HD**0.5
    heads_local = query_local.shape[1]

    def step_fn(state, item):
        block, first = item
        top, total, acc = state
        cols = first + jnp.arange(width, dtype=jnp.int32)
        seen = mask_fn(cols)
        parts = block.reshape(width, heads_local, 2, HD)
        scores = (
            jnp.einsum(
                "tgqd,ngd->gqtn", query_local, parts[:, :, 0], preferred_element_type=jnp.float32
            )
            * scale
        )
        scores = jnp.where(seen, scores, -1e30)
        new_top = jnp.maximum(top, jnp.max(scores, axis=-1))
        factor = jnp.exp(top - new_top)
        weights = jnp.where(seen, jnp.exp(scores - new_top[..., None]), 0.0)
        total = total * factor + jnp.sum(weights, axis=-1)
        acc = acc * factor[..., None] + jnp.einsum(
            "gqtn,ngd->gqtd",
            weights.astype(jnp.bfloat16),
            parts[:, :, 1],
            preferred_element_type=jnp.float32,
        )
        return ((new_top, total, acc), None)

    firsts = jnp.arange(steps, dtype=jnp.int32) * width
    state, _ = lax.scan(step_fn, carry, (keys.reshape(steps, width, keys.shape[1]), firsts))
    return state


def per_device(queries, own_kv, retain, anchor_hidden, w_kv):
    tok = queries.shape[0]
    heads_local = w_kv.shape[1] // (2 * HD)
    group = H // KVH
    host = lax.axis_index("hst")
    query_local = queries.reshape(tok, heads_local, group, HD)
    anchor_kv = jnp.dot(
        lax.all_gather(anchor_hidden, ("hst", "tensor"), axis=0, tiled=True),
        w_kv,
        preferred_element_type=jnp.float32,
    ).astype(jnp.bfloat16)
    kept = jnp.take(own_kv, retain[:, 0], axis=0)
    all_kept = lax.all_gather(kept, "hst", axis=0, tiled=True)
    start_state = (
        jnp.full((heads_local, group, tok), -1e30, jnp.float32),
        jnp.zeros((heads_local, group, tok), jnp.float32),
        jnp.zeros((heads_local, group, tok, HD), jnp.float32),
    )
    rows = jnp.arange(tok, dtype=jnp.int32)
    kept_rows = retain.shape[0]

    def all_seen(cols):
        return jnp.ones((1, cols.shape[0]), bool)

    def causal(cols):
        return cols[None, :] <= rows[:, None]

    def earlier(cols):
        return (cols // kept_rows < host)[None, :]

    state = attend(start_state, query_local, anchor_kv, all_seen)
    state = attend(state, query_local, own_kv, causal)
    top, total, acc = attend(state, query_local, all_kept, earlier)
    result = acc / total[..., None]
    result = jnp.transpose(result, (2, 0, 1, 3)).reshape(tok, heads_local * group * HD)
    return result.astype(jnp.bfloat16)


def solution(mesh):
    placed = (
        P("hst", "tensor"),
        P("hst", "tensor"),
        P("hst", "tensor"),
        P(("hst", "tensor"), None),
        P(None, "tensor"),
    )
    return jax.shard_map(
        per_device, mesh=mesh, in_specs=placed, out_specs=P("hst", "tensor"), check_vma=False
    )
```

profile of v0, /device:TPU:17, one launch (start us, length us, event | category | flops | bytes accessed | tf_op | source)
XLA Modules:
  0.0 263.6 jit_solution(3129388676653762799)
XLA Ops:
  8.0 1.6 gather_fusion
  11.1 1.9 copy.37
  13.0 2.3 copy.34
  15.3 1.6 copy.36
  16.9 6.2 %fusion.35 = (f32[8,512]{1,0:T(8,128)S(1)}, f32[512,512,8]{1,0,2:T(8,128)}) fusion(pred[512,512]{0,1:T(8,128)(4,1)S(1)} %iota_compare_fusion, bf16[512,1,2,128]{0,3,2,1:T(8,128)(2,1)} %bitcast.264, bf16[512,1024]{1,0:T(8,128)(2,1)} %param.9), kind=kOutput, calls=%fused_computation.59 | convolution fusion | flops 543158272 | bytes 9846784 | tf_op jit(solution)/shard_map/while/body/eval_jaxpr/tgqd,ngd->gqtn/dot_general | solution.py:25
  23.1 116.0 %all-gather.6.cloned.1.call-done = bf16[256,4,8192]{2,1,0:T(4,128)(2,1)} async-done(((bf16[1,4,8192]{2,1,0:T(4,128)(2,1)}), bf16[256,4,8192]{2,1,0:T(4,128)(2,1)}) %all-gather.6.cloned.1.call-update) | async-done | bytes 16777232 | tf_op jit(solution)/shard_map/all_gather | solution.py:55
  139.1 23.6 %reshape.164 = bf16[1024,8192]{1,0:T(8,128)(2,1)} reshape(bf16[256,4,8192]{2,1,0:T(4,128)(2,1)} %all-gather.6.cloned.1.call-done) | data formatting | bytes 33554432
  162.8 12.2 %convolution_convert_fusion = bf16[1024,256]{1,0:T(8,128)(2,1)} fusion(bf16[1024,8192]{1,0:T(8,128)(2,1)} %reshape.164, bf16[8192,256]{1,0:T(8,128)(2,1)} %param.13), kind=kOutput, calls=%fused_computation.67 | convolution fusion | flops 4295229440 | bytes 21495808 | tf_op jit(solution)/shard_map/dot_general | solution.py:54
  175.0 15.9 %while.38 = (s32[]{:T(128)}, f32[1,8,512]{2,1,0:T(8,128)S(1)}, f32[1,8,512]{2,1,0:T(8,128)S(1)}, f32[1,8,512,128]{3,2,1,0:T(8,128)S(1)}, bf16[2,512,256]{2,1,0:T...) while((s32[]{:T(128)}, f32[1,8,512]{2,1,0:T(8,128)S(1)}, ...), condition=%wide.region_3.4_spmd.clone, body=%wide.region_0.3_spmd.clone.sunk | while | flops 1092116480 | bytes 31981676 | solution.py:44
  175.0 1.7 constant_dynamic-slice_fusion.5
  179.1 1.4 fusion.69
  180.5 2.4 bitcast_add_fusion.13
  183.0 1.7 constant_dynamic-slice_fusion.5
  187.0 1.4 fusion.69
  188.4 2.4 bitcast_add_fusion.13
  190.9 4.7 %fusion.37 = f32[8,512]{1,0:T(8,128)S(1)} fusion(f32[512,512,8]{1,0,2:T(8,128)} %get-tuple-element.256, f32[8,512]{1,0:T(8,128)S(1)} %bitcast.260, pred[512,512]{0,1:T(8,128)(4,1)} %copy-done), kind=kLoop, calls=%fused_computation.61 | loop fusion | flops 10481664 | bytes 8683520 | tf_op jit(solution)/shard_map/while/body/eval_jaxpr/reduce_sum | solution.py:34
  195.7 7.5 %bitcast_add_fusion.4 = f32[1,8,512,128]{3,2,1,0:T(8,128)} fusion(f32[1,8,512,128]{3,2,1,0:T(8,128)S(1)} %get-tuple-element.165, f32[512,512,8]{1,0,2:T(8,128)} %get-tuple-element.256, f32[8,512]{1,0:T(8,128)S(1)} %bitcast.261, pred[512,512]{0,1:T(8,128)(4,1)S(1)} %copy-done.1, f32[8,512]{1,0:T(8,128)S(1)} %get-tuple-element.249, ...), kind=kOutput, calls=%fused_computation.65 | convolution fusion | flops 548405248 | bytes 13008896 | tf_op jit(solution)/shard_map/while/body/eval_jaxpr/gqtn,ngd->gqtd/dot_general | solution.py:35
  203.2 49.6 %while.37 = (s32[]{:T(128)}, f32[1,8,512]{2,1,0:T(8,128)S(1)}, f32[1,8,512]{2,1,0:T(8,128)S(1)}, f32[1,8,512,128]{3,2,1,0:T(8,128)}, s32[4]{0:T(128)S(1)}, /*ind...) while((s32[]{:T(128)}, f32[1,8,512]{2,1,0:T(8,128)S(1)}, ...), condition=%wide.region_9.10_spmd, body=%wide.region_6.9_spmd.sunk | while | flops 1102074368 | bytes 48761524 | solution.py:44
  205.6 2.2 bitcast_reduce_fusion.4
  207.8 2.4 fusion.66
  210.3 4.0 %bitcast_add_fusion.11 = f32[1,8,512,128]{3,2,1,0:T(8,128)S(1)} fusion(f32[1,8,512,128]{3,2,1,0:T(8,128)S(1)} %copy-done.2, f32[512,512,8]{1,0,2:T(8,128)S(1)} %get-tuple-element.347, f32[8,512]{1,0:T(8,128)S(1)} %bitcast.256, pred[512]{0:T(512)(128)(4,1)S(1)} %fusion.64, f32[8,512]{1,0:T(8,128)S(1)} %get-tuple-element.348, ...), kind=kOutput, calls=%fused_computation.12.clone.1 | convolution fusion | flops 548405248 | bytes 12747776 | tf_op jit(solution)/shard_map/while/body/eval_jaxpr/gqtn,ngd->gqtd/dot_general | solution.py:35
  214.3 1.3 copy-done.3
  218.0 2.2 bitcast_reduce_fusion.4
  220.2 2.4 fusion.66
  222.7 4.0 %bitcast_add_fusion.11 = f32[1,8,512,128]{3,2,1,0:T(8,128)S(1)} fusion(f32[1,8,512,128]{3,2,1,0:T(8,128)S(1)} %copy-done.2, f32[512,512,8]{1,0,2:T(8,128)S(1)} %get-tuple-element.347, f32[8,512]{1,0:T(8,128)S(1)} %bitcast.256, pred[512]{0:T(512)(128)(4,1)S(1)} %fusion.64, f32[8,512]{1,0:T(8,128)S(1)} %get-tuple-element.348, ...), kind=kOutput, calls=%fused_computation.12.clone.1 | convolution fusion | flops 548405248 | bytes 12747776 | tf_op jit(solution)/shard_map/while/body/eval_jaxpr/gqtn,ngd->gqtd/dot_general | solution.py:35
  230.4 2.2 bitcast_reduce_fusion.4
  232.6 2.4 fusion.66
  235.0 4.0 %bitcast_add_fusion.11 = f32[1,8,512,128]{3,2,1,0:T(8,128)S(1)} fusion(f32[1,8,512,128]{3,2,1,0:T(8,128)S(1)} %copy-done.2, f32[512,512,8]{1,0,2:T(8,128)S(1)} %get-tuple-element.347, f32[8,512]{1,0:T(8,128)S(1)} %bitcast.256, pred[512]{0:T(512)(128)(4,1)S(1)} %fusion.64, f32[8,512]{1,0:T(8,128)S(1)} %get-tuple-element.348, ...), kind=kOutput, calls=%fused_computation.12.clone.1 | convolution fusion | flops 548405248 | bytes 12747776 | tf_op jit(solution)/shard_map/while/body/eval_jaxpr/gqtn,ngd->gqtd/dot_general | solution.py:35
  242.8 2.2 bitcast_reduce_fusion.4
  245.0 2.4 fusion.66
  247.4 4.0 %bitcast_add_fusion.11 = f32[1,8,512,128]{3,2,1,0:T(8,128)S(1)} fusion(f32[1,8,512,128]{3,2,1,0:T(8,128)S(1)} %copy-done.2, f32[512,512,8]{1,0,2:T(8,128)S(1)} %get-tuple-element.347, f32[8,512]{1,0:T(8,128)S(1)} %bitcast.256, pred[512]{0:T(512)(128)(4,1)S(1)} %fusion.64, f32[8,512]{1,0:T(8,128)S(1)} %get-tuple-element.348, ...), kind=kOutput, calls=%fused_computation.12.clone.1 | convolution fusion | flops 548405248 | bytes 12747776 | tf_op jit(solution)/shard_map/while/body/eval_jaxpr/gqtn,ngd->gqtd/dot_general | solution.py:35
  252.8 2.0 fusion.47
  (77 shorter events, 23.1 us)
Async XLA Ops:
  6.5 132.6 %all-gather.6.cloned.1.call-start = ((), (), s32[]{:S(2)}) async-start(), calls=%async_computation.1 | async-start | bytes 16842752 | tf_op jit(solution)/shard_map/all_gather | solution.py:55
  7.3 196.0 %all-gather.4.cloned.1.call-start = ((), (), s32[]{:S(2)}) async-start(), calls=%async_computation | async-start | bytes 1081344 | tf_op jit(solution)/shard_map/all_gather | solution.py:60
  11.1 151.7 %copy-start = (pred[512,512]{0,1:T(8,128)(4,1)}, pred[512,512]{0,1:T(8,128)(4,1)S(1)}, u32[]{:S(2)}) copy-start(pred[512,512]{0,1:T(8,128)(4,1)S(1)} %iota_compare_fusion) | copy-start | bytes 786436
  190.9 4.8 %copy-start.1 = (pred[512,512]{0,1:T(8,128)(4,1)S(1)}, pred[512,512]{0,1:T(8,128)(4,1)}, u32[]{:S(2)}) copy-start(pred[512,512]{0,1:T(8,128)(4,1)} %copy-done) | copy-start | bytes 786436
  190.9 4.8 %copy-start.4 = (bf16[512,256]{0,1:T(8,128)(2,1)S(1)}, bf16[512,256]{0,1:T(8,128)(2,1)}, u32[]{:S(2)}) copy-start(bf16[512,256]{0,1:T(8,128)(2,1)} %copy.37) | copy-start | bytes 786436
  205.6 4.6 %copy-start.2 = (f32[1,8,512,128]{3,2,1,0:T(8,128)S(1)}, f32[1,8,512,128]{3,2,1,0:T(8,128)}, u32[]{:S(2)}) copy-start(f32[1,8,512,128]{3,2,1,0:T(8,128)} %get-tuple-element.395) | copy-start | bytes 6291460 | tf_op jit(solution)/shard_map/while
  214.3 1.3 copy-start.3
  218.0 4.6 %copy-start.2 = (f32[1,8,512,128]{3,2,1,0:T(8,128)S(1)}, f32[1,8,512,128]{3,2,1,0:T(8,128)}, u32[]{:S(2)}) copy-start(f32[1,8,512,128]{3,2,1,0:T(8,128)} %get-tuple-element.395) | copy-start | bytes 6291460 | tf_op jit(solution)/shard_map/while
  226.7 1.3 copy-start.3
  230.4 4.6 %copy-start.2 = (f32[1,8,512,128]{3,2,1,0:T(8,128)S(1)}, f32[1,8,512,128]{3,2,1,0:T(8,128)}, u32[]{:S(2)}) copy-start(f32[1,8,512,128]{3,2,1,0:T(8,128)} %get-tuple-element.395) | copy-start | bytes 6291460 | tf_op jit(solution)/shard_map/while
  239.1 1.3 copy-start.3
  242.8 4.6 %copy-start.2 = (f32[1,8,512,128]{3,2,1,0:T(8,128)S(1)}, f32[1,8,512,128]{3,2,1,0:T(8,128)}, u32[]{:S(2)}) copy-start(f32[1,8,512,128]{3,2,1,0:T(8,128)} %get-tuple-element.395) | copy-start | bytes 6291460 | tf_op jit(solution)/shard_map/while
  251.5 1.3 copy-start.3
Sparse Core Ops, SparseCore 0:
  11.0 128.1 all-gather.5
  141.7 44.5 all-gather.3
where the time goes:
time: 266 us; the launch traced here: 264 us
  waiting for transfers between devices  117 us (44%)
  matrix products  58.2 us (22%)
  local copies, waits for them, and re-layouts  50.5 us (19%)
  other arithmetic  24.1 us (9%)
  between operations  13.5 us (5%)
    all_gather x1, waiting for transfers between devices, per_device(): lax.all_gather(anchor_hidden, ('hst', 'tensor'), axis=0, tiled=True)  116 us
    unnamed x11, local copies, waits for them, and re-layouts  30.6 us
    dot_general x7, matrix products, step_fn(): jnp.einsum('gqtn,ngd->gqtd', weights.astype(jnp.bfloat16), parts[:, :, 1]...  28.5 us
    dot_general x7, matrix products, step_fn(): jnp.einsum('tgqd,ngd->gqtn', query_local, parts[:, :, 0], preferred_eleme...  17.5 us
    reduce_sum x7, other arithmetic, step_fn(): total = total * factor + jnp.sum(weights, axis=-1)  17.2 us
    dynamic_slice x16, local copies, waits for them, and re-layouts, attend(): lax.scan(step_fn, carry, (keys.reshape(steps, width, keys.shape[1]), firs...  12.3 us
    dot_general x1, matrix products, per_device(): jnp.dot(lax.all_gather(anchor_hidden, ('hst', 'tensor'), axis=0, tiled=Tr...  12.2 us
  transfers between devices with their start and end apart: 2, of which 1 were waited for; matrix products, arithmetic and copies ran while one was open for 30% of the time, Pallas kernels for 0%

commit v1 on v0

v1 whole, which is shorter than its diff:
```python
import functools

import jax
import jax.numpy as jnp
from jax import lax
from jax.experimental import pallas as pl
from jax.experimental.pallas import tpu as pltpu
from jax.sharding import PartitionSpec as P

H = 64
KVH = 8
HD = 128
GROUP = H // KVH
EXP2_SCALE = 1.4426950408889634 / HD**0.5
AUG = HD + 16
KEY_BLOCK = 256
KEPT_BLOCK = 512
SAFE_TOTAL = 2.0**100


def mul_nt(a, b):
    return lax.dot_general(a, b, (((1,), (1,)), ((), ())), preferred_element_type=jnp.float32)


def mul(a, b):
    return lax.dot_general(a, b, (((1,), (0,)), ((), ())), preferred_element_type=jnp.float32)


def weights_of(scores, top):
    return jnp.exp2((scores - top) * EXP2_SCALE).astype(jnp.bfloat16)


def head_cols(head):
    return pl.ds(pl.multiple_of(head * HD, HD), HD)


def fill_values(vt_ref, kv_ref):
    vt_ref[:HD, :] = kv_ref[:, HD:].T
    vt_ref[HD:, :] = jnp.ones((AUG - HD, vt_ref.shape[1]), jnp.bfloat16)


def select_kernel(retain_ref, own_ref, out_ref):
    tok = own_ref.shape[0]
    picks = retain_ref[...] == lax.broadcasted_iota(jnp.int32, (retain_ref.shape[0], tok), 1)
    kept = mul(jnp.where(picks, 1.0, 0.0).astype(jnp.bfloat16), own_ref[...]).astype(jnp.bfloat16)
    for copy in range(out_ref.shape[0]):
        out_ref[copy] = kept


def project_kernel(rows_ref, w_ref, out_ref):
    rows = jnp.concatenate([rows_ref[i] for i in range(rows_ref.shape[0])], axis=0)
    part = mul(rows, w_ref[...]).astype(jnp.bfloat16)
    for copy in range(out_ref.shape[0]):
        out_ref[copy] = part


def own_kernel(q_ref, kv_ref, top_ref, acc_ref, vt_ref):
    tok = q_ref.shape[0]
    fill_values(vt_ref, kv_ref)
    keys = lax.broadcasted_iota(jnp.int32, (KEY_BLOCK, KEY_BLOCK), 0)
    queries = lax.broadcasted_iota(jnp.int32, (KEY_BLOCK, KEY_BLOCK), 1)
    seen = keys <= queries

    def one_head(head):
        for block in range(tok // KEY_BLOCK):
            at = slice(block * KEY_BLOCK, (block + 1) * KEY_BLOCK)
            q = q_ref[at, head_cols(head)]
            parts = [
                mul_nt(kv_ref[i * KEY_BLOCK : (i + 1) * KEY_BLOCK, :HD], q) for i in range(block + 1)
            ]
            parts[-1] = jnp.where(seen, parts[-1], -1e30)
            top = functools.reduce(
                jnp.maximum, [jnp.max(part, axis=0, keepdims=True) for part in parts]
            )
            acc = None
            for i, part in enumerate(parts):
                term = mul(vt_ref[:, i * KEY_BLOCK : (i + 1) * KEY_BLOCK], weights_of(part, top))
                acc = term if acc is None else acc + term
            top_ref[pl.ds(head, 1), at] = top
            acc_ref[pl.ds(head, 1), :, at] = acc[None]

    def step(i, carry):
        one_head(2 * i)
        one_head(2 * i + 1)
        return carry

    lax.fori_loop(0, GROUP // 2, step, 0)


def careful_block(q, keys, values, valid, top, acc):
    scores = mul_nt(keys, q)
    if valid is not None:
        scores = jnp.where(valid, scores, -1e30)
    new_top = jnp.maximum(top, jnp.max(scores, axis=0, keepdims=True))
    weights = weights_of(scores, new_top)
    return new_top, acc * jnp.exp2((top - new_top) * EXP2_SCALE) + mul(values, weights)


def kept_kernel(count_ref, q_ref, kv_ref, top_ref, acc_ref, new_top_ref, new_acc_ref, vt_ref):
    count = count_ref[0]
    blocks = lax.div(count + KEPT_BLOCK - 1, KEPT_BLOCK)
    fill_values(vt_ref, kv_ref)
    spare = lax.broadcasted_iota(jnp.int32, vt_ref.shape, 1) >= count
    vt_ref[...] = jnp.where(spare, 0.0, vt_ref[...]).astype(jnp.bfloat16)
    new_top_ref[...] = top_ref[...]
    new_acc_ref[...] = acc_ref[...]

    def one_head(head, first):
        q = q_ref[:, head_cols(head)]
        top = top_ref[pl.ds(head, 1), :]
        acc = new_acc_ref[head]
        for i in range(KEPT_BLOCK // KEY_BLOCK):
            at = pl.ds(pl.multiple_of(first + i * KEY_BLOCK, KEY_BLOCK), KEY_BLOCK)
            weights = weights_of(mul_nt(kv_ref[at, :HD], q), top)
            acc = acc + mul(vt_ref[:, at], weights)
        new_acc_ref[head] = acc

    def step(i, carry):
        first = lax.div(i, GROUP // 2) * KEPT_BLOCK
        head = lax.rem(i, GROUP // 2) * 2
        one_head(head, first)
        one_head(head + 1, first)
        return carry

    lax.fori_loop(0, blocks * (GROUP // 2), step, 0)
    totals = new_acc_ref[:, HD : HD + 8, :]
    safe = jnp.all(totals < SAFE_TOTAL)

    @pl.when(jnp.logical_not(safe))
    def careful():
        def head_step(head, carry):
            q = q_ref[:, head_cols(head)]
            new_top_ref[pl.ds(head, 1), :] = top_ref[pl.ds(head, 1), :]
            new_acc_ref[head] = acc_ref[head]

            def block_step(block, carry):
                at = pl.ds(pl.multiple_of(block * KEY_BLOCK, KEY_BLOCK), KEY_BLOCK)
                valid = (
                    lax.broadcasted_iota(jnp.int32, (KEY_BLOCK, 1), 0) + block * KEY_BLOCK < count
                )
                top, acc = careful_block(
                    q,
                    kv_ref[at, :HD],
                    vt_ref[:, at],
                    valid,
                    new_top_ref[pl.ds(head, 1), :],
                    new_acc_ref[head],
                )
                new_top_ref[pl.ds(head, 1), :] = top
                new_acc_ref[head] = acc
                return carry

            return lax.fori_loop(0, blocks * (KEPT_BLOCK // KEY_BLOCK), block_step, carry)

        lax.fori_loop(0, GROUP, head_step, 0)


def anchor_kernel(q_ref, kv_ref, top_ref, acc_ref, out_ref, vt_ref, total_ref):
    fill_values(vt_ref, kv_ref)
    steps = kv_ref.shape[0] // KEY_BLOCK

    def finish(head, acc):
        result = acc[:HD] * (1.0 / acc[HD : HD + 1])
        out_ref[:, head_cols(head)] = result.T.astype(jnp.bfloat16)

    def one_head(head):
        q = q_ref[:, head_cols(head)]
        top = top_ref[pl.ds(head, 1), :]
        acc = acc_ref[head]
        for i in range(steps):
            at = slice(i * KEY_BLOCK, (i + 1) * KEY_BLOCK)
            acc = acc + mul(vt_ref[:, at], weights_of(mul_nt(kv_ref[at, :HD], q), top))
        total_ref[pl.ds(head, 1), :] = acc[HD : HD + 1]
        finish(head, acc)

    def step(i, carry):
        one_head(2 * i)
        one_head(2 * i + 1)
        return carry

    lax.fori_loop(0, GROUP // 2, step, 0)
    safe = jnp.all(total_ref[...] < SAFE_TOTAL)

    @pl.when(jnp.logical_not(safe))
    def careful():
        def head_step(head, carry):
            q = q_ref[:, head_cols(head)]
            top, acc = top_ref[pl.ds(head, 1), :], acc_ref[head]
            for i in range(steps):
                at = slice(i * KEY_BLOCK, (i + 1) * KEY_BLOCK)
                top, acc = careful_block(q, kv_ref[at, :HD], vt_ref[:, at], None, top, acc)
            finish(head, acc)
            return carry

        lax.fori_loop(0, GROUP, head_step, 0)


VMEM = pl.BlockSpec(memory_space=pltpu.VMEM)
SMEM = pl.BlockSpec(memory_space=pltpu.SMEM)


def call(kernel, name, in_specs, outs, args, scratch=(), flops=0, nbytes=0, limit=32):
    return pl.pallas_call(
        kernel,
        in_specs=in_specs,
        out_specs=[VMEM] * len(outs),
        out_shape=[jax.ShapeDtypeStruct(shape, dtype) for shape, dtype in outs],
        scratch_shapes=list(scratch),
        compiler_params=pltpu.CompilerParams(vmem_limit_bytes=limit << 20),
        cost_estimate=pl.CostEstimate(flops=flops, bytes_accessed=nbytes, transcendentals=0),
        name=name,
    )(*args)


def per_device(queries, own_kv, retain, anchor_hidden, w_kv):
    tok, width = own_kv.shape
    hosts = lax.axis_size("hst")
    heads = lax.axis_size("tensor")
    host = lax.axis_index("hst")
    kept_rows = retain.shape[0]
    rows = anchor_hidden.shape[0]
    bf16, f32 = jnp.bfloat16, jnp.float32

    with jax.named_scope("gather_hidden"):
        hidden = jnp.broadcast_to(anchor_hidden[None], (heads, *anchor_hidden.shape))
        hidden = lax.all_to_all(hidden, "tensor", 0, 0)
    with jax.named_scope("select_kept"):
        (kept,) = call(
            select_kernel,
            "select",
            [VMEM] * 2,
            [((hosts, kept_rows, width), bf16)],
            (retain, own_kv),
            flops=2 * kept_rows * tok * width,
            nbytes=2 * hosts * kept_rows * width,
        )
        kept = lax.all_to_all(kept, "hst", 0, 0).reshape(hosts * kept_rows, width)
    with jax.named_scope("own"):
        top, acc = call(
            own_kernel,
            "own",
            [VMEM] * 2,
            [((GROUP, tok), f32), ((GROUP, AUG, tok), f32)],
            (queries, own_kv),
            [pltpu.VMEM((AUG, tok), bf16)],
            flops=4 * GROUP * tok * tok * HD,
            nbytes=4 << 20,
        )
    with jax.named_scope("project"):
        (part,) = call(
            project_kernel,
            "project",
            [VMEM] * 2,
            [((hosts, heads * rows, width), bf16)],
            (hidden, w_kv),
            flops=2 * heads * rows * w_kv.shape[0] * width,
            nbytes=5 << 20,
        )
        anchor = lax.all_to_all(part, "hst", 0, 0).reshape(hosts * heads * rows, width)
    with jax.named_scope("kept"):
        top, acc = call(
            kept_kernel,
            "kept",
            [SMEM] + [VMEM] * 4,
            [((GROUP, tok), f32), ((GROUP, AUG, tok), f32)],
            ((host * kept_rows)[None].astype(jnp.int32), queries, kept, top, acc),
            [pltpu.VMEM((AUG, hosts * kept_rows), bf16)],
            flops=4 * GROUP * tok * hosts * kept_rows * HD,
            nbytes=8 << 20,
        )
    with jax.named_scope("anchor"):
        (out,) = call(
            anchor_kernel,
            "anchor",
            [VMEM] * 4,
            [((tok, GROUP * HD), bf16)],
            (queries, anchor, top, acc),
            [pltpu.VMEM((AUG, anchor.shape[0]), bf16), pltpu.VMEM((GROUP, tok), f32)],
            flops=4 * GROUP * tok * anchor.shape[0] * HD,
            nbytes=5 << 20,
        )
    return out


def solution(mesh):
    placed = (
        P("hst", "tensor"),
        P("hst", "tensor"),
        P("hst", "tensor"),
        P(("hst", "tensor"), None),
        P(None, "tensor"),
    )
    return jax.shard_map(
        per_device, mesh=mesh, in_specs=placed, out_specs=P("hst", "tensor"), check_vma=False
    )
```

time: 266 us -> 139 us (0.52)
  the two profiles are of different devices: /device:TPU:17 before, /device:TPU:25 now
where the time goes in v1:
time: 139 us
  Pallas kernels  81.9 us (59%)
  waiting for transfers between devices  26.2 us (19%)
  starting transfers between devices  21.8 us (16%)
  local copies, waits for them, and re-layouts  8.73 us (6%)
    pallas_call x5, Pallas kernels, call(): pl.pallas_call(kernel, in_specs=in_specs, out_specs=[VMEM] * len(outs), o...  81.9 us
    all_to_all x1, waiting for transfers between devices, per_device(): hidden = lax.all_to_all(hidden, 'tensor', 0, 0)  15 us
    all_to_all x1, waiting for transfers between devices, per_device(): kept = lax.all_to_all(kept, 'hst', 0, 0).reshape(hosts * kept_rows, width)  11.2 us
    all_to_all x1, starting transfers between devices, per_device(): hidden = lax.all_to_all(hidden, 'tensor', 0, 0)  8.19 us
    all_to_all x1, starting transfers between devices, per_device(): kept = lax.all_to_all(kept, 'hst', 0, 0).reshape(hosts * kept_rows, width)  7.48 us
    unnamed x13, local copies, waits for them, and re-layouts  6.96 us
    all_to_all x1, starting transfers between devices, per_device(): lax.all_to_all(part, 'hst', 0, 0).reshape(hosts * heads * rows, width)  6.14 us
  transfers between devices with their start and end apart: 3, of which 2 were waited for; matrix products, arithmetic and copies ran while one was open for 1% of the time, Pallas kernels for 42%

profile of v1, /device:TPU:25, one launch (start us, length us, event | category | flops | bytes accessed | tf_op | source)
XLA Modules:
  0.0 138.7 jit_solution(18300252653087070013)
XLA Ops:
  0.0 1.8 %broadcast_in_dim.4 = bf16[8,4,8192]{2,1,0:T(4,128)(2,1)} broadcast(bf16[4,8192]{1,0:T(4,128)(2,1)} %param.8), dimensions={1,2} | broadcast | bytes 589824 | tf_op jit(solution)/shard_map/gather_hidden/broadcast_in_dim | solution.py:225
  1.8 8.2 %all-to-all-start = ((bf16[8,4,8192]{2,1,0:T(4,128)(2,1)}), bf16[8,4,8192]{2,1,0:T(4,128)(2,1)S(1)}, u32[]{:S(2)}, u32[]{:S(2)}) async-start(bf16[8,4,8192]{2,1,0:T(4,128)(2,1)} %broadcast_in_dim.4), calls=%async_computation | async-start | bytes 1048576 | tf_op jit(solution)/shard_map/gather_hidden/all_to_all | solution.py:226
  10.0 0.7 copy.6.retain_ref
  10.7 0.0 copy-start.1
  10.7 0.9 copy-done.1
  11.7 1.3 select.1
  12.9 15.0 %all-to-all-done.rows_ref = bf16[8,4,8192]{2,1,0:T(4,128)(2,1)S(1)} async-done(((bf16[8,4,8192]{2,1,0:T(4,128)(2,1)}), bf16[8,4,8192]{2,1,0:T(4,128)(2,1)S(1)}, u32[]{:S(2)}, u32[]{:S(2)}) %all-to-all-start) | async-done | bytes 524320 | tf_op jit(solution)/shard_map/gather_hidden/all_to_all | solution.py:226
  27.9 7.5 %all-to-all-start.2 = ((bf16[32,64,256]{2,1,0:T(8,128)(2,1)}), bf16[32,64,256]{2,1,0:T(8,128)(2,1)S(1)}, u32[]{:S(2)}, u32[]{:S(2)}) async-start(bf16[32,64,256]{2,1,0:T(8,128)(2,1)} %select.1), calls=%async_computation.2 | async-start | bytes 2097152 | tf_op jit(solution)/shard_map/select_kept/all_to_all | solution.py:237
  35.4 0.0 copy-start
  35.4 2.2 %copy-done = bf16[8192,256]{1,0:T(8,128)(2,1)S(1)} copy-done((bf16[8192,256]{1,0:T(8,128)(2,1)S(1)}, bf16[8192,256]{1,0:T(8,128)(2,1)}, u32[]{:S(2)}) %copy-start) | copy-done | bytes 4194328
  37.6 0.0 copy-start.2
  37.6 0.0 copy-start.3
  37.6 1.7 %project.1 = bf16[32,32,256]{2,1,0:T(8,128)(2,1)} custom-call(bf16[8,4,8192]{2,1,0:T(4,128)(2,1)S(1)} %all-to-all-done.rows_ref, bf16[8192,256]{1,0:T(8,128)(2,1)S(1)} %copy-done), custom_call_target="tpu_custom_call" | custom-call | flops 134217728 | bytes 5242880 | tf_op jit(solution)/shard_map/project/project/pallas_call | solution.py:203
  39.3 11.2 %all-to-all-done.2 = bf16[32,64,256]{2,1,0:T(8,128)(2,1)S(1)} async-done(((bf16[32,64,256]{2,1,0:T(8,128)(2,1)}), bf16[32,64,256]{2,1,0:T(8,128)(2,1)S(1)}, u32[]{:S(2)}, u32[]{:S(2)}) %all-to-all-start.2) | async-done | bytes 1048608 | tf_op jit(solution)/shard_map/select_kept/all_to_all | solution.py:237
  50.5 6.1 %all-to-all-start.1 = ((bf16[32,32,256]{2,1,0:T(8,128)(2,1)}), bf16[32,32,256]{2,1,0:T(8,128)(2,1)S(1)}, u32[]{:S(2)}, u32[]{:S(2)}) async-start(bf16[32,32,256]{2,1,0:T(8,128)(2,1)} %project.1), calls=%async_computation.1 | async-start | bytes 1048576 | tf_op jit(solution)/shard_map/project/all_to_all | solution.py:259
  56.6 0.0 copy-done.2
  56.7 0.0 copy-done.3
  56.7 4.7 %own.1 = (f32[8,512]{1,0:T(8,128)S(1)}, f32[8,144,512]{2,1,0:T(8,128)S(1)}) custom-call(bf16[512,1024]{1,0:T(8,128)(2,1)S(1)} %copy-done.3, bf16[512,256]{1,0:T(8,128)(2,1)S(1)} %copy-done.2), custom_call_target="tpu_custom_call" | custom-call | flops 1073741824 | bytes 4194304 | tf_op jit(solution)/shard_map/own/own/pallas_call | solution.py:203
  61.4 51.1 %kept.1 = (f32[8,512]{1,0:T(8,128)S(1)}, f32[8,144,512]{2,1,0:T(8,128)S(1)}) custom-call(s32[1]{0:T(128)} %bitcast.1.count_ref, bf16[512,1024]{1,0:T(8,128)(2,1)S(1)} %copy-done.3, bf16[2048,256]{1,0:T(8,128)(2,1)S(1)} %bitcast.3, f32[8,512]{1,0:T(8,128)S(1)} %get-tuple-element.9.top_ref, f32[8,144,512]{2,1,0:T(8,128)S(1)} %get-tuple-element.10.acc_ref), custom_call_target="tpu_custom_call" | custom-call | flops 4294967296 | bytes 8388608 | tf_op jit(solution)/shard_map/kept/kept/pallas_call | solution.py:203
  112.5 0.0 copy-start.4
  112.5 1.4 %copy-done.4 = f32[8,144,512]{2,1,0:T(8,128)} copy-done((f32[8,144,512]{2,1,0:T(8,128)}, f32[8,144,512]{2,1,0:T(8,128)S(1)}, u32[]{:S(2)}) %copy-start.4) | copy-done | bytes 2359320
  113.9 0.0 all-to-all-done.1
  113.9 0.0 copy-start.5
  113.9 1.7 %copy-done.5 = f32[8,144,512]{2,1,0:T(8,128)S(1)} copy-done((f32[8,144,512]{2,1,0:T(8,128)S(1)}, f32[8,144,512]{2,1,0:T(8,128)}, u32[]{:S(2)}) %copy-start.5) | copy-done | bytes 2359320
  115.6 23.1 %anchor.1 = bf16[512,1024]{1,0:T(8,128)(2,1)} custom-call(bf16[512,1024]{1,0:T(8,128)(2,1)S(1)} %copy-done.3, bf16[1024,256]{1,0:T(8,128)(2,1)S(1)} %bitcast.4, f32[8,512]{1,0:T(8,128)S(1)} %get-tuple-element.11.top_ref, f32[8,144,512]{2,1,0:T(8,128)S(1)} %copy-done.5), custom_call_target="tpu_custom_call" | custom-call | flops 2147483648 | bytes 5242880 | tf_op jit(solution)/shard_map/anchor/anchor/pallas_call | solution.py:203
Async XLA Ops:
  1.8 26.1 %all-to-all-start = ((bf16[8,4,8192]{2,1,0:T(4,128)(2,1)}), bf16[8,4,8192]{2,1,0:T(4,128)(2,1)S(1)}, u32[]{:S(2)}, u32[]{:S(2)}) async-start(bf16[8,4,8192]{2,1,0:T(4,128)(2,1)} %broadcast_in_dim.4), calls=%async_computation | async-start | bytes 1048576 | tf_op jit(solution)/shard_map/gather_hidden/all_to_all | solution.py:226
  10.7 0.9 copy-start.1
  27.9 22.6 %all-to-all-start.2 = ((bf16[32,64,256]{2,1,0:T(8,128)(2,1)}), bf16[32,64,256]{2,1,0:T(8,128)(2,1)S(1)}, u32[]{:S(2)}, u32[]{:S(2)}) async-start(bf16[32,64,256]{2,1,0:T(8,128)(2,1)} %select.1), calls=%async_computation.2 | async-start | bytes 2097152 | tf_op jit(solution)/shard_map/select_kept/all_to_all | solution.py:237
  35.4 2.2 %copy-start = (bf16[8192,256]{1,0:T(8,128)(2,1)S(1)}, bf16[8192,256]{1,0:T(8,128)(2,1)}, u32[]{:S(2)}) copy-start(bf16[8192,256]{1,0:T(8,128)(2,1)} %w_ref.1) | copy-start | bytes 12582916
  37.6 19.0 %copy-start.2 = (bf16[512,256]{1,0:T(8,128)(2,1)S(1)}, bf16[512,256]{1,0:T(8,128)(2,1)}, u32[]{:S(2)}) copy-start(bf16[512,256]{1,0:T(8,128)(2,1)} %kv_ref.1) | copy-start | bytes 786436
  37.6 19.1 %copy-start.3 = (bf16[512,1024]{1,0:T(8,128)(2,1)S(1)}, bf16[512,1024]{1,0:T(8,128)(2,1)}, u32[]{:S(2)}) copy-start(bf16[512,1024]{1,0:T(8,128)(2,1)} %q_ref.5) | copy-start | bytes 3145732
  50.5 63.5 %all-to-all-start.1 = ((bf16[32,32,256]{2,1,0:T(8,128)(2,1)}), bf16[32,32,256]{2,1,0:T(8,128)(2,1)S(1)}, u32[]{:S(2)}, u32[]{:S(2)}) async-start(bf16[32,32,256]{2,1,0:T(8,128)(2,1)} %project.1), calls=%async_computation.1 | async-start | bytes 1048576 | tf_op jit(solution)/shard_map/project/all_to_all | solution.py:259
  112.5 1.4 %copy-start.4 = (f32[8,144,512]{2,1,0:T(8,128)}, f32[8,144,512]{2,1,0:T(8,128)S(1)}, u32[]{:S(2)}) copy-start(f32[8,144,512]{2,1,0:T(8,128)S(1)} %get-tuple-element.12.acc_ref) | copy-start | bytes 7077892
  113.9 1.7 %copy-start.5 = (f32[8,144,512]{2,1,0:T(8,128)S(1)}, f32[8,144,512]{2,1,0:T(8,128)}, u32[]{:S(2)}) copy-start(f32[8,144,512]{2,1,0:T(8,128)} %copy-done.4) | copy-start | bytes 7077892

commit v2 on v1

v2 whole, which is shorter than its diff:
```python
import functools

import jax
import jax.numpy as jnp
from jax import lax
from jax.experimental import pallas as pl
from jax.experimental.pallas import tpu as pltpu
from jax.sharding import PartitionSpec as P

H = 64
KVH = 8
HD = 128
GROUP = H // KVH
EXP2_SCALE = 1.4426950408889634 / HD**0.5
AUG = HD + 16
KEY_BLOCK = 256
KEPT_BLOCK = 1024
SIDE = 4
HEAD_STEP = 4
SAFE_TOTAL = 2.0**100


def mul_nt(a, b):
    return lax.dot_general(a, b, (((1,), (1,)), ((), ())), preferred_element_type=jnp.float32)


def mul(a, b):
    return lax.dot_general(a, b, (((1,), (0,)), ((), ())), preferred_element_type=jnp.float32)


def weights_of(scores, top):
    return jnp.exp2((scores - top) * EXP2_SCALE).astype(jnp.bfloat16)


def weighted(vt_ref, first, weights):
    total = None
    for i, block in enumerate(weights):
        at = pl.ds(first + i * KEY_BLOCK, KEY_BLOCK)
        if not isinstance(first, int):
            at = pl.ds(pl.multiple_of(first + i * KEY_BLOCK, KEY_BLOCK), KEY_BLOCK)
        term = mul(vt_ref[:, at], block)
        total = term if total is None else total + term
    return total


def head_cols(head):
    if isinstance(head, int):
        return slice(head * HD, (head + 1) * HD)
    return pl.ds(pl.multiple_of(head * HD, HD), HD)


def fill_values(vt_ref, kv_ref):
    vt_ref[:HD, :] = kv_ref[:, HD:].T
    vt_ref[HD:, :] = jnp.ones((AUG - HD, vt_ref.shape[1]), jnp.bfloat16)


def start_all(pairs, sem):
    copies = [pltpu.make_async_copy(src, dst, sem.at[i]) for i, (src, dst) in enumerate(pairs)]
    for copy in copies:
        copy.start()
    return copies


def wait_all(copies):
    for copy in copies:
        copy.wait()


def repeat_kernel(rows_hbm, out_hbm, rows_ref, load_sem, sem):
    wait_all(start_all([(rows_hbm, rows_ref)], load_sem))
    wait_all(start_all([(rows_ref, out_hbm.at[i]) for i in range(out_hbm.shape[0])], sem))


def select_kernel(retain_hbm, own_hbm, kept_hbm, retain_ref, kv_ref, kept_ref, sem):
    load = start_all([(own_hbm, kv_ref), (retain_hbm, retain_ref)], sem)
    tok, kept_rows = kv_ref.shape[0], kept_ref.shape[0]
    load[1].wait()
    picks = retain_ref[...] == lax.broadcasted_iota(jnp.int32, (tok, kept_rows), 0)
    picks = jnp.where(picks, 1.0, 0.0).astype(jnp.bfloat16)
    load[0].wait()
    kept_ref[...] = lax.dot_general(
        picks, kv_ref[...], (((0,), (0,)), ((), ())), preferred_element_type=jnp.float32
    ).astype(jnp.bfloat16)
    wait_all(start_all([(kept_ref, kept_hbm)], sem))


def project_kernel(rows_ref, w_ref, out_hbm, part_ref, sem):
    rows = jnp.concatenate([rows_ref[i] for i in range(rows_ref.shape[0])], axis=0)
    part_ref[...] = mul(rows, w_ref[...]).astype(jnp.bfloat16)
    wait_all(start_all([(part_ref, out_hbm.at[i]) for i in range(out_hbm.shape[0])], sem))


def own_kernel(q_ref, kv_ref, stat_ref, acc_ref, vt_ref):
    tok = kv_ref.shape[0]
    fill_values(vt_ref, kv_ref)
    keys = lax.broadcasted_iota(jnp.int32, (KEY_BLOCK, KEY_BLOCK), 0)
    queries = lax.broadcasted_iota(jnp.int32, (KEY_BLOCK, KEY_BLOCK), 1)
    seen = keys <= queries

    def one_head(head):
        for block in range(tok // KEY_BLOCK):
            at = slice(block * KEY_BLOCK, (block + 1) * KEY_BLOCK)
            q = q_ref[at, head_cols(head)]
            parts = [
                mul_nt(kv_ref[i * KEY_BLOCK : (i + 1) * KEY_BLOCK, :HD], q) for i in range(block + 1)
            ]
            parts[-1] = jnp.where(seen, parts[-1], -1e30)
            top = functools.reduce(
                jnp.maximum, [jnp.max(part, axis=0, keepdims=True) for part in parts]
            )
            weights = [weights_of(part, top) for part in parts]
            acc = weighted(vt_ref, 0, weights)
            stat_ref[0, pl.ds(head, 1), at] = top
            stat_ref[1, pl.ds(head, 1), at] = acc[HD : HD + 1]
            acc_ref[head, :, at] = acc[:HD].astype(jnp.bfloat16)

    def step(i, carry):
        for part in range(HEAD_STEP):
            one_head(HEAD_STEP * i + part)
        return carry

    lax.fori_loop(0, GROUP // HEAD_STEP, step, 0)


def fast_rows(q_ref, kv_ref, vt_ref, stat_ref, head, first, rows):
    q = q_ref[:, head_cols(head)]
    top = stat_ref[0, pl.ds(head, 1), :]
    weights = []
    for i in range(rows // KEY_BLOCK):
        at = pl.ds(first + i * KEY_BLOCK, KEY_BLOCK)
        if not isinstance(first, int):
            at = pl.ds(pl.multiple_of(first + i * KEY_BLOCK, KEY_BLOCK), KEY_BLOCK)
        weights.append(weights_of(mul_nt(kv_ref[at, :HD], q), top))
    return weighted(vt_ref, first, weights)


def careful_rows(q_ref, kv_ref, vt_ref, stat_ref, acc_ref, head, count):
    q = q_ref[:, head_cols(head)]

    def block_step(block, carry):
        top, acc = carry
        at = pl.ds(pl.multiple_of(block * KEY_BLOCK, KEY_BLOCK), KEY_BLOCK)
        row = lax.broadcasted_iota(jnp.int32, (KEY_BLOCK, 1), 0) + block * KEY_BLOCK
        scores = jnp.where(row < count, mul_nt(kv_ref[at, :HD], q), -1e30)
        new_top = jnp.maximum(top, jnp.max(scores, axis=0, keepdims=True))
        term = mul(vt_ref[:, at], weights_of(scores, new_top))
        return new_top, acc * jnp.exp2((top - new_top) * EXP2_SCALE) + term

    total = jnp.broadcast_to(stat_ref[1, pl.ds(head, 1), :], (AUG - HD, q.shape[0]))
    acc = jnp.concatenate([acc_ref[head].astype(jnp.float32), total], axis=0)
    return lax.fori_loop(
        0, kv_ref.shape[0] // KEY_BLOCK, block_step, (stat_ref[0, pl.ds(head, 1), :], acc)
    )


def kept_kernel(
    at_ref,
    q_ref,
    mine_hbm,
    other_hbm,
    stat_ref,
    acc_ref,
    new_stat_ref,
    new_acc_ref,
    mine_ref,
    other_ref,
    sum_ref,
    kv_ref,
    vt_ref,
    sem,
):
    load = start_all([(mine_hbm, mine_ref), (other_hbm, other_ref)], sem)
    for head in range(GROUP):
        sum_ref[head, :HD] = acc_ref[head].astype(jnp.float32)
        sum_ref[head, HD:] = jnp.broadcast_to(
            stat_ref[1, head : head + 1, :], (AUG - HD, sum_ref.shape[2])
        )
    wait_all(load)
    host = at_ref[0]
    chip, core = lax.div(host, 2), lax.rem(host, 2)
    senders, kept_rows, _ = mine_ref.shape
    count = host * kept_rows
    for piece in range(senders):
        y = lax.rem(lax.div(chip, SIDE) + SIDE - piece // SIDE, SIDE)
        x = lax.rem(lax.rem(chip, SIDE) + SIDE - piece % SIDE, SIDE)
        first = (y * SIDE + x) * 2 * kept_rows
        for ref, which in ((mine_ref, core), (other_ref, 1 - core)):
            at = pl.multiple_of(first + which * kept_rows, kept_rows)
            kv_ref[pl.ds(at, kept_rows), :] = ref[piece]
    fill_values(vt_ref, kv_ref)
    spare = lax.broadcasted_iota(jnp.int32, vt_ref.shape, 1) >= count
    vt_ref[...] = jnp.where(spare, 0.0, vt_ref[...]).astype(jnp.bfloat16)
    steps = GROUP // HEAD_STEP

    def step(i, carry):
        first = lax.div(i, steps) * KEPT_BLOCK
        for part in range(HEAD_STEP):
            head = lax.rem(i, steps) * HEAD_STEP + part
            sum_ref[head] += fast_rows(q_ref, kv_ref, vt_ref, stat_ref, head, first, KEPT_BLOCK)
        return carry

    lax.fori_loop(0, lax.div(count + KEPT_BLOCK - 1, KEPT_BLOCK) * steps, step, 0)
    new_stat_ref[0] = stat_ref[0]
    for head in range(GROUP):
        new_acc_ref[head] = sum_ref[head, :HD].astype(jnp.bfloat16)
        new_stat_ref[1, head : head + 1, :] = sum_ref[head, HD : HD + 1]
    safe = jnp.all(new_stat_ref[1] < SAFE_TOTAL)

    @pl.when(jnp.logical_not(safe))
    def careful():
        def head_step(head, carry):
            top, acc = careful_rows(q_ref, kv_ref, vt_ref, stat_ref, acc_ref, head, count)
            new_stat_ref[0, pl.ds(head, 1), :] = top
            new_stat_ref[1, pl.ds(head, 1), :] = acc[HD : HD + 1]
            new_acc_ref[head] = acc[:HD].astype(jnp.bfloat16)
            return carry

        lax.fori_loop(0, GROUP, head_step, 0)


def anchor_kernel(q_ref, kv_ref, stat_ref, acc_ref, out_ref, vt_ref, total_ref):
    fill_values(vt_ref, kv_ref)
    rows = kv_ref.shape[0]

    def finish(head, acc, total):
        out_ref[:, head_cols(head)] = (acc * (1.0 / total)).T.astype(jnp.bfloat16)

    for head in range(GROUP):
        term = fast_rows(q_ref, kv_ref, vt_ref, stat_ref, head, 0, rows)
        total = stat_ref[1, head : head + 1, :] + term[HD : HD + 1]
        total_ref[head : head + 1, :] = total
        finish(head, acc_ref[head].astype(jnp.float32) + term[:HD], total)
    safe = jnp.all(total_ref[...] < SAFE_TOTAL)

    @pl.when(jnp.logical_not(safe))
    def careful():
        def head_step(head, carry):
            _, acc = careful_rows(q_ref, kv_ref, vt_ref, stat_ref, acc_ref, head, rows)
            finish(head, acc[:HD], acc[HD : HD + 1])
            return carry

        lax.fori_loop(0, GROUP, head_step, 0)


VMEM = pl.BlockSpec(memory_space=pltpu.VMEM)
SMEM = pl.BlockSpec(memory_space=pltpu.SMEM)


HBM = pl.BlockSpec(memory_space=pltpu.HBM)


def call(kernel, name, in_specs, outs, args, scratch=(), flops=0, nbytes=0, limit=24, out_spec=VMEM):
    return pl.pallas_call(
        kernel,
        in_specs=in_specs,
        out_specs=[out_spec] * len(outs),
        out_shape=[jax.ShapeDtypeStruct(shape, dtype) for shape, dtype in outs],
        scratch_shapes=list(scratch),
        compiler_params=pltpu.CompilerParams(vmem_limit_bytes=limit << 20),
        cost_estimate=pl.CostEstimate(flops=flops, bytes_accessed=nbytes, transcendentals=0),
        name=name,
    )(*args)


def moves(dy, dx, dcore=0):
    pairs = []
    for y in range(SIDE):
        for x in range(SIDE):
            for core in range(2):
                to = ((y + dy) % SIDE * SIDE + (x + dx) % SIDE) * 2 + (core ^ dcore)
                pairs.append(((y * SIDE + x) * 2 + core, to))
    return pairs


def per_device(queries, own_kv, retain, anchor_hidden, w_kv):
    tok, width = own_kv.shape
    hosts = lax.axis_size("hst")
    heads = lax.axis_size("tensor")
    host = lax.axis_index("hst")
    kept_rows = retain.shape[0]
    rows = anchor_hidden.shape[0]
    bf16, f32 = jnp.bfloat16, jnp.float32
    state = [((2, GROUP, tok), f32), ((GROUP, HD, tok), bf16)]
    barrier = lax.optimization_barrier

    dma = pltpu.SemaphoreType.DMA
    with jax.named_scope("gather_hidden"):
        (hidden,) = call(
            repeat_kernel,
            "repeat",
            [HBM],
            [((heads, *anchor_hidden.shape), bf16)],
            (anchor_hidden,),
            [pltpu.VMEM(anchor_hidden.shape, bf16), dma((1,)), dma((heads,))],
            nbytes=1 << 20,
            limit=63,
            out_spec=HBM,
        )
        hidden, own_kv, queries, retain = barrier((hidden, own_kv, queries, retain))
        hidden = lax.all_to_all(hidden, "tensor", 0, 0)
    with jax.named_scope("select_kept"):
        (kept,) = call(
            select_kernel,
            "select",
            [HBM] * 2,
            [((kept_rows, width), bf16)],
            (retain.T, own_kv),
            [
                pltpu.VMEM((1, kept_rows), jnp.int32),
                pltpu.VMEM((tok, width), bf16),
                pltpu.VMEM((kept_rows, width), bf16),
                dma((2,)),
            ],
            flops=2 * kept_rows * tok * width,
            nbytes=1 << 18,
            limit=63,
            out_spec=HBM,
        )
        kept, own_kv, queries = barrier((kept, own_kv, queries))
        row = [kept] + [lax.ppermute(kept, "hst", moves(0, d)) for d in range(1, SIDE)]

    with jax.named_scope("own"):
        stat, acc = call(
            own_kernel,
            "own",
            [VMEM, VMEM],
            state,
            (queries, own_kv),
            [pltpu.VMEM((AUG, tok), bf16)],
            nbytes=1 << 10,
        )
    with jax.named_scope("kept_rows"):
        *row, stat, acc = barrier((*row, stat, acc))
        row = jnp.stack(row)
        plane = [row] + [lax.ppermute(row, "hst", moves(d, 0)) for d in range(1, SIDE)]
    with jax.named_scope("project"):
        hidden, row, stat, acc = barrier((hidden, row, stat, acc))
        (part,) = call(
            project_kernel,
            "project",
            [VMEM] * 2,
            [((hosts, heads * rows, width), bf16)],
            (hidden, w_kv),
            [pltpu.VMEM((heads * rows, width), bf16), dma((hosts,))],
            flops=2 * heads * rows * w_kv.shape[0] * width,
            nbytes=5 << 20,
            out_spec=HBM,
        )
        _, *plane = barrier((part, *plane))
        anchor = lax.all_to_all(part, "hst", 0, 0).reshape(hosts * heads * rows, width)
        mine = jnp.concatenate(plane)
        other = lax.ppermute(mine, "hst", moves(0, 0, 1))
    with jax.named_scope("kept"):
        stat, acc = call(
            kept_kernel,
            "kept",
            [SMEM, VMEM, HBM, HBM, VMEM, VMEM],
            state,
            (host[None].astype(jnp.int32), queries, mine, other, stat, acc),
            [
                pltpu.VMEM(mine.shape, bf16),
                pltpu.VMEM(mine.shape, bf16),
                pltpu.VMEM((GROUP, AUG, tok), f32),
                pltpu.VMEM((hosts * kept_rows, width), bf16),
                pltpu.VMEM((AUG, hosts * kept_rows), bf16),
                dma((2,)),
            ],
            nbytes=1 << 10,
        )
    with jax.named_scope("anchor"):
        (out,) = call(
            anchor_kernel,
            "anchor",
            [VMEM] * 4,
            [((tok, GROUP * HD), bf16)],
            (queries, anchor, stat, acc),
            [pltpu.VMEM((AUG, anchor.shape[0]), bf16), pltpu.VMEM((GROUP, tok), f32)],
            nbytes=1 << 20,
        )
    return out


def solution(mesh):
    placed = (
        P("hst", "tensor"),
        P("hst", "tensor"),
        P("hst", "tensor"),
        P(("hst", "tensor"), None),
        P(None, "tensor"),
    )
    return jax.shard_map(
        per_device, mesh=mesh, in_specs=placed, out_specs=P("hst", "tensor"), check_vma=False
    )
```

time: 139 us -> 108 us (0.78)
  the two profiles are of different devices: /device:TPU:25 before, /device:TPU:17 now
where the time goes in v2:
time: 108 us; the launch traced here: 107 us
  Pallas kernels  73.6 us (68%)
  starting transfers between devices  22.5 us (21%)
  local copies, waits for them, and re-layouts  7.47 us (7%)
  waiting for transfers between devices  2.57 us (2%)
    pallas_call x6, Pallas kernels, call(): pl.pallas_call(kernel, in_specs=in_specs, out_specs=[out_spec] * len(outs...  73.6 us
    all_to_all x1, starting transfers between devices, per_device(): hidden = lax.all_to_all(hidden, 'tensor', 0, 0)  8.2 us
    unnamed x19, local copies, waits for them, and re-layouts  7.46 us
    all_to_all x1, starting transfers between devices, per_device(): lax.all_to_all(part, 'hst', 0, 0).reshape(hosts * heads * rows, width)  6.75 us
    ppermute x3, starting transfers between devices, per_device(): lax.ppermute(kept, 'hst', moves(0, d))  3.68 us
    ppermute x3, starting transfers between devices, per_device(): lax.ppermute(row, 'hst', moves(d, 0))  2.87 us
    all_to_all x1, waiting for transfers between devices, per_device(): hidden = lax.all_to_all(hidden, 'tensor', 0, 0)  2.55 us
  transfers between devices with their start and end apart: 9, of which 1 were waited for; matrix products, arithmetic and copies ran while one was open for 1% of the time, Pallas kernels for 46%

profile of v2, /device:TPU:17, one launch (start us, length us, event | category | flops | bytes accessed | tf_op | source)
XLA Modules:
  0.0 107.1 jit_solution(3688434204690583322)
XLA Ops:
  0.0 1.7 %repeat.1 = bf16[8,4,8192]{2,1,0:T(4,128)(2,1)} custom-call(bf16[4,8192]{1,0:T(4,128)(2,1)} %rows_hbm.1), custom_call_target="tpu_custom_call" | custom-call | bytes 1048576 | tf_op jit(solution)/shard_map/gather_hidden/repeat/pallas_call | solution.py:253
  1.7 8.2 %all-to-all-start = ((bf16[8,4,8192]{2,1,0:T(4,128)(2,1)}), bf16[8,4,8192]{2,1,0:T(4,128)(2,1)S(1)}, u32[]{:S(2)}, u32[]{:S(2)}) async-start(bf16[8,4,8192]{2,1,0:T(4,128)(2,1)} %repeat.1), calls=%async_computation | async-start | bytes 1048576 | tf_op jit(solution)/shard_map/gather_hidden/all_to_all | solution.py:300
  9.9 1.8 %select.1 = bf16[64,256]{1,0:T(8,128)(2,1)} custom-call(s32[1,64]{1,0:T(1,128)} %bitcast.12, bf16[512,256]{1,0:T(8,128)(2,1)} %kv_ref), custom_call_target="tpu_custom_call" | custom-call | flops 16777216 | bytes 262144 | tf_op jit(solution)/shard_map/select_kept/select/pallas_call | solution.py:253
  11.7 2.6 %collective-permute-start.2 = (bf16[64,256]{1,0:T(8,128)(2,1)}, bf16[64,256]{1,0:T(8,128)(2,1)S(1)}, u32[]{:S(2)}, u32[]{:S(2)}) collective-permute-start(bf16[64,256]{1,0:T(8,128)(2,1)} %select.1), channel_id=1, source_target_pairs={{0,48},{8,56},{16,0},{24,8},{32,16},{40,24},{48,32},{56,40},{64,11... | collective-permute-start | bytes 98312 | tf_op jit(solution)/shard_map/select_kept/ppermute | solution.py:320
  14.3 0.5 collective-permute-start.1
  14.8 0.6 collective-permute-start
  15.4 1.2 %copy-done = bf16[512,1024]{1,0:T(8,128)(2,1)S(1)} copy-done((bf16[512,1024]{1,0:T(8,128)(2,1)S(1)}, bf16[512,1024]{1,0:T(8,128)(2,1)}, u32[]{:S(2)}) %copy-start) | copy-done | bytes 1048600
  16.6 0.9 copy-done.3
  17.6 4.0 %own.1 = (f32[2,8,512]{2,1,0:T(8,128)S(1)}, bf16[8,128,512]{2,1,0:T(8,128)(2,1)S(1)}) custom-call(bf16[512,1024]{1,0:T(8,128)(2,1)S(1)} %copy-done, bf16[512,256]{1,0:T(8,128)(2,1)S(1)} %copy-done.3), custom_call_target="tpu_custom_call" | custom-call | bytes 1024 | tf_op jit(solution)/shard_map/own/own/pallas_call | solution.py:253
  21.6 0.0 copy-start.4
  21.6 0.0 collective-permute-done.2
  21.6 0.0 collective-permute-done.1
  21.6 0.0 collective-permute-done
  21.6 0.8 pad_maximum_fusion
  22.5 0.2 collective-permute-start.5
  22.7 2.6 %collective-permute-start.4 = (bf16[4,64,256]{2,1,0:T(8,128)(2,1)S(1)}, bf16[4,64,256]{2,1,0:T(8,128)(2,1)S(1)}, u32[]{:S(2)}, u32[]{:S(2)}) collective-permute-start(bf16[4,64,256]{2,1,0:T(8,128)(2,1)S(1)} %pad_maximum_fusion), channel_id=1, source_target_pairs={{0,128},{8,136},{16,144},{24,152},{32,160},{40,168},{48,176},{56,1... | collective-permute-start | bytes 393224 | tf_op jit(solution)/shard_map/kept_rows/ppermute | solution.py:335
  25.3 0.0 collective-permute-start.3
  25.3 2.5 %all-to-all-done.rows_ref = bf16[8,4,8192]{2,1,0:T(4,128)(2,1)S(1)} async-done(((bf16[8,4,8192]{2,1,0:T(4,128)(2,1)}), bf16[8,4,8192]{2,1,0:T(4,128)(2,1)S(1)}, u32[]{:S(2)}, u32[]{:S(2)}) %all-to-all-start) | async-done | bytes 524320 | tf_op jit(solution)/shard_map/gather_hidden/all_to_all | solution.py:300
  27.9 2.2 %copy-done.2 = bf16[8192,256]{1,0:T(8,128)(2,1)S(1)} copy-done((bf16[8192,256]{1,0:T(8,128)(2,1)S(1)}, bf16[8192,256]{1,0:T(8,128)(2,1)}, u32[]{:S(2)}) %copy-start.2) | copy-done | bytes 4194328
  30.1 1.9 %project.1 = bf16[32,32,256]{2,1,0:T(8,128)(2,1)} custom-call(bf16[8,4,8192]{2,1,0:T(4,128)(2,1)S(1)} %all-to-all-done.rows_ref, bf16[8192,256]{1,0:T(8,128)(2,1)S(1)} %copy-done.2), custom_call_target="tpu_custom_call" | custom-call | flops 134217728 | bytes 5242880 | tf_op jit(solution)/shard_map/project/project/pallas_call | solution.py:253
  32.0 0.0 collective-permute-done.5
  32.0 0.0 collective-permute-done.4
  32.0 0.0 collective-permute-done.3
  32.1 1.0 collective-permute-start.6
  33.1 6.7 %all-to-all-start.1 = ((bf16[32,32,256]{2,1,0:T(8,128)(2,1)}), bf16[32,32,256]{2,1,0:T(8,128)(2,1)S(1)}, u32[]{:S(2)}, u32[]{:S(2)}) async-start(bf16[32,32,256]{2,1,0:T(8,128)(2,1)} %project.1), calls=%async_computation.1 | async-start | bytes 1048576 | tf_op jit(solution)/shard_map/project/all_to_all | solution.py:350
  39.8 0.0 collective-permute-done.6.other_hbm
  39.9 0.8 copy-done.6
  40.7 1.2 %copy-done.5 = bf16[8,128,512]{2,1,0:T(8,128)(2,1)S(1)} copy-done((bf16[8,128,512]{2,1,0:T(8,128)(2,1)S(1)}, bf16[8,128,512]{2,1,0:T(8,128)(2,1)}, u32[]{:S(2)}) %copy-start.5) | copy-done | bytes 1048600
  41.9 1.0 copy-done.7
  42.9 41.9 %kept.1 = (f32[2,8,512]{2,1,0:T(8,128)S(1)}, bf16[8,128,512]{2,1,0:T(8,128)(2,1)S(1)}) custom-call(s32[1]{0:T(128)} %bitcast.6.at_ref, bf16[512,1024]{1,0:T(8,128)(2,1)S(1)} %copy-done.1, bf16[16,64,256]{2,1,0:T(8,128)(2,1)S(1)} %constant_dynamic-update-slice_fusion.mine_hbm, bf16[16,64,256]{2,1,0:T(8,128)(2,1)S(1)} %copy-done.7, ...), custom_call_target="tpu_custom_call" | custom-call | bytes 1024 | tf_op jit(solution)/shard_map/kept/kept/pallas_call | solution.py:253
  84.8 0.0 all-to-all-done.1
  84.8 22.3 %anchor.1 = bf16[512,1024]{1,0:T(8,128)(2,1)} custom-call(bf16[512,1024]{1,0:T(8,128)(2,1)S(1)} %copy-done.1, bf16[1024,256]{1,0:T(8,128)(2,1)S(1)} %bitcast.7, f32[2,8,512]{2,1,0:T(8,128)S(1)} %get-tuple-element.51.stat_ref, bf16[8,128,512]{2,1,0:T(8,128)(2,1)S(1)} %get-tuple-element.52.acc_ref), custom_call_target="tpu_custom_call" | custom-call | bytes 1048576 | tf_op jit(solution)/shard_map/anchor/anchor/pallas_call | solution.py:253
  (13 shorter events, 0.1 us)
Async XLA Ops:
  1.7 26.2 %all-to-all-start = ((bf16[8,4,8192]{2,1,0:T(4,128)(2,1)}), bf16[8,4,8192]{2,1,0:T(4,128)(2,1)S(1)}, u32[]{:S(2)}, u32[]{:S(2)}) async-start(bf16[8,4,8192]{2,1,0:T(4,128)(2,1)} %repeat.1), calls=%async_computation | async-start | bytes 1048576 | tf_op jit(solution)/shard_map/gather_hidden/all_to_all | solution.py:300
  11.7 9.9 %collective-permute-start.2 = (bf16[64,256]{1,0:T(8,128)(2,1)}, bf16[64,256]{1,0:T(8,128)(2,1)S(1)}, u32[]{:S(2)}, u32[]{:S(2)}) collective-permute-start(bf16[64,256]{1,0:T(8,128)(2,1)} %select.1), channel_id=1, source_target_pairs={{0,48},{8,56},{16,0},{24,8},{32,16},{40,24},{48,32},{56,40},{64,11... | collective-permute-start | bytes 98312 | tf_op jit(solution)/shard_map/select_kept/ppermute | solution.py:320
  14.3 7.4 %collective-permute-start.1 = (bf16[64,256]{1,0:T(8,128)(2,1)}, bf16[64,256]{1,0:T(8,128)(2,1)S(1)}, u32[]{:S(2)}, u32[]{:S(2)}) collective-permute-start(bf16[64,256]{1,0:T(8,128)(2,1)} %select.1), channel_id=1, source_target_pairs={{0,32},{8,40},{16,48},{24,56},{32,0},{40,8},{48,16},{56,24},{64,96... | collective-permute-start | bytes 98312 | tf_op jit(solution)/shard_map/select_kept/ppermute | solution.py:320
  14.8 6.9 %collective-permute-start = (bf16[64,256]{1,0:T(8,128)(2,1)}, bf16[64,256]{1,0:T(8,128)(2,1)S(1)}, u32[]{:S(2)}, u32[]{:S(2)}) collective-permute-start(bf16[64,256]{1,0:T(8,128)(2,1)} %select.1), channel_id=1, source_target_pairs={{0,16},{8,24},{16,32},{24,40},{32,48},{40,56},{48,0},{56,8},{64,80... | collective-permute-start | bytes 98312 | tf_op jit(solution)/shard_map/select_kept/ppermute | solution.py:320
  15.4 1.2 %copy-start = (bf16[512,1024]{1,0:T(8,128)(2,1)S(1)}, bf16[512,1024]{1,0:T(8,128)(2,1)}, u32[]{:S(2)}) copy-start(bf16[512,1024]{1,0:T(8,128)(2,1)} %q_ref.2) | copy-start | bytes 3145732
  16.6 0.9 copy-start.3
  17.6 23.1 %copy-start.1 = (bf16[512,1024]{1,0:T(8,128)(2,1)S(1)}, bf16[512,1024]{1,0:T(8,128)(2,1)}, u32[]{:S(2)}) copy-start(bf16[512,1024]{1,0:T(8,128)(2,1)} %q_ref.2) | copy-start | bytes 3145732
  21.6 11.5 %copy-start.4 = (bf16[8,128,512]{2,1,0:T(8,128)(2,1)}, bf16[8,128,512]{2,1,0:T(8,128)(2,1)S(1)}, u32[]{:S(2)}) copy-start(bf16[8,128,512]{2,1,0:T(8,128)(2,1)S(1)} %get-tuple-element.50.acc_ref) | copy-start | bytes 3145732
  22.5 9.5 %collective-permute-start.5 = (bf16[4,64,256]{2,1,0:T(8,128)(2,1)S(1)}, bf16[4,64,256]{2,1,0:T(8,128)(2,1)S(1)}, u32[]{:S(2)}, u32[]{:S(2)}) collective-permute-start(bf16[4,64,256]{2,1,0:T(8,128)(2,1)S(1)} %pad_maximum_fusion), channel_id=1, source_target_pairs={{0,192},{8,200},{16,208},{24,216},{32,224},{40,232},{48,240},{56,2... | collective-permute-start | bytes 393224 | tf_op jit(solution)/shard_map/kept_rows/ppermute | solution.py:335
  22.7 9.3 %collective-permute-start.4 = (bf16[4,64,256]{2,1,0:T(8,128)(2,1)S(1)}, bf16[4,64,256]{2,1,0:T(8,128)(2,1)S(1)}, u32[]{:S(2)}, u32[]{:S(2)}) collective-permute-start(bf16[4,64,256]{2,1,0:T(8,128)(2,1)S(1)} %pad_maximum_fusion), channel_id=1, source_target_pairs={{0,128},{8,136},{16,144},{24,152},{32,160},{40,168},{48,176},{56,1... | collective-permute-start | bytes 393224 | tf_op jit(solution)/shard_map/kept_rows/ppermute | solution.py:335
  25.3 6.7 %collective-permute-start.3 = (bf16[4,64,256]{2,1,0:T(8,128)(2,1)S(1)}, bf16[4,64,256]{2,1,0:T(8,128)(2,1)S(1)}, u32[]{:S(2)}, u32[]{:S(2)}) collective-permute-start(bf16[4,64,256]{2,1,0:T(8,128)(2,1)S(1)} %pad_maximum_fusion), channel_id=1, source_target_pairs={{0,64},{8,72},{16,80},{24,88},{32,96},{40,104},{48,112},{56,120},{... | collective-permute-start | bytes 393224 | tf_op jit(solution)/shard_map/kept_rows/ppermute | solution.py:335
  27.9 2.2 %copy-start.2 = (bf16[8192,256]{1,0:T(8,128)(2,1)S(1)}, bf16[8192,256]{1,0:T(8,128)(2,1)}, u32[]{:S(2)}) copy-start(bf16[8192,256]{1,0:T(8,128)(2,1)} %w_ref.1) | copy-start | bytes 12582916
  32.1 7.8 %collective-permute-start.6 = (bf16[16,64,256]{2,1,0:T(8,128)(2,1)S(1)}, bf16[16,64,256]{2,1,0:T(8,128)(2,1)S(1)}, u32[]{:S(2)}, u32[]{:S(2)}) collective-permute-start(bf16[16,64,256]{2,1,0:T(8,128)(2,1)S(1)} %constant_dynamic-update-slice_fusion.mine_hbm), channel_id=1, source_target_pairs={{0,8},{8,0},{16,24},{24,16},{32,40},{40,32},{48,56},{56,48},{64,72... | collective-permute-start | bytes 1572872 | tf_op jit(solution)/shard_map/project/ppermute | solution.py:352
  33.1 51.7 %all-to-all-start.1 = ((bf16[32,32,256]{2,1,0:T(8,128)(2,1)}), bf16[32,32,256]{2,1,0:T(8,128)(2,1)S(1)}, u32[]{:S(2)}, u32[]{:S(2)}) async-start(bf16[32,32,256]{2,1,0:T(8,128)(2,1)} %project.1), calls=%async_computation.1 | async-start | bytes 1048576 | tf_op jit(solution)/shard_map/project/all_to_all | solution.py:350
  39.9 0.8 copy-start.6
  40.7 1.2 %copy-start.5 = (bf16[8,128,512]{2,1,0:T(8,128)(2,1)S(1)}, bf16[8,128,512]{2,1,0:T(8,128)(2,1)}, u32[]{:S(2)}) copy-start(bf16[8,128,512]{2,1,0:T(8,128)(2,1)} %copy-done.4) | copy-start | bytes 3145732
  41.9 1.0 copy-start.7

commit v3 on v2

--- a/solution.py
+++ b/solution.py
@@ -16,6 +16,7 @@
 KEY_BLOCK = 256
 KEPT_BLOCK = 1024
 SIDE = 4
+OWN_FIRST = 6
 HEAD_STEP = 4
 SAFE_TOTAL = 2.0**100
 
@@ -67,8 +68,15 @@
 
 
 def repeat_kernel(rows_hbm, out_hbm, rows_ref, load_sem, sem):
-    wait_all(start_all([(rows_hbm, rows_ref)], load_sem))
-    wait_all(start_all([(rows_ref, out_hbm.at[i]) for i in range(out_hbm.shape[0])], sem))
+    half = rows_hbm.shape[1] // 2
+    parts = [slice(0, half), slice(half, 2 * half)]
+    load = start_all([(rows_hbm.at[:, at], rows_ref.at[:, at]) for at in parts], load_sem)
+    store = []
+    for part, at in enumerate(parts):
+        load[part].wait()
+        pairs = [(rows_ref.at[:, at], out_hbm.at[i, :, at]) for i in range(out_hbm.shape[0])]
+        store += start_all(pairs, sem.at[part])
+    wait_all(store)
 
 
 def select_kernel(retain_hbm, own_hbm, kept_hbm, retain_ref, kv_ref, kept_ref, sem):
@@ -84,23 +92,22 @@
     wait_all(start_all([(kept_ref, kept_hbm)], sem))
 
 
-def project_kernel(rows_ref, w_ref, out_hbm, part_ref, sem):
+def project_kernel(rows_ref, w_ref, out_ref):
     rows = jnp.concatenate([rows_ref[i] for i in range(rows_ref.shape[0])], axis=0)
-    part_ref[...] = mul(rows, w_ref[...]).astype(jnp.bfloat16)
-    wait_all(start_all([(part_ref, out_hbm.at[i]) for i in range(out_hbm.shape[0])], sem))
-
-
-def own_kernel(q_ref, kv_ref, stat_ref, acc_ref, vt_ref):
+    out_ref[...] = mul(rows, w_ref[...]).astype(jnp.bfloat16)
+
+
+def own_kernel(first, heads, q_ref, kv_ref, stat_ref, acc_ref, vt_ref):
     tok = kv_ref.shape[0]
     fill_values(vt_ref, kv_ref)
     keys = lax.broadcasted_iota(jnp.int32, (KEY_BLOCK, KEY_BLOCK), 0)
     queries = lax.broadcasted_iota(jnp.int32, (KEY_BLOCK, KEY_BLOCK), 1)
     seen = keys <= queries
 
-    def one_head(head):
+    for head in range(heads):
         for block in range(tok // KEY_BLOCK):
             at = slice(block * KEY_BLOCK, (block + 1) * KEY_BLOCK)
-            q = q_ref[at, head_cols(head)]
+            q = q_ref[at, head_cols(first + head)]
             parts = [
                 mul_nt(kv_ref[i * KEY_BLOCK : (i + 1) * KEY_BLOCK, :HD], q) for i in range(block + 1)
             ]
@@ -108,18 +115,10 @@
             top = functools.reduce(
                 jnp.maximum, [jnp.max(part, axis=0, keepdims=True) for part in parts]
             )
-            weights = [weights_of(part, top) for part in parts]
-            acc = weighted(vt_ref, 0, weights)
-            stat_ref[0, pl.ds(head, 1), at] = top
-            stat_ref[1, pl.ds(head, 1), at] = acc[HD : HD + 1]
+            acc = weighted(vt_ref, 0, [weights_of(part, top) for part in parts])
+            stat_ref[0, head : head + 1, at] = top
+            stat_ref[1, head : head + 1, at] = acc[HD : HD + 1]
             acc_ref[head, :, at] = acc[:HD].astype(jnp.bfloat16)
-
-    def step(i, carry):
-        for part in range(HEAD_STEP):
-            one_head(HEAD_STEP * i + part)
-        return carry
-
-    lax.fori_loop(0, GROUP // HEAD_STEP, step, 0)
 
 
 def fast_rows(q_ref, kv_ref, vt_ref, stat_ref, head, first, rows):
@@ -156,26 +155,29 @@
 def kept_kernel(
     at_ref,
     q_ref,
-    mine_hbm,
-    other_hbm,
-    stat_ref,
-    acc_ref,
+    mine_ref,
+    other_ref,
+    stat_a_ref,
+    acc_a_ref,
+    stat_b_ref,
+    acc_b_ref,
     new_stat_ref,
     new_acc_ref,
-    mine_ref,
-    other_ref,
+    stat_ref,
+    own_ref,
     sum_ref,
     kv_ref,
     vt_ref,
-    sem,
 ):
-    load = start_all([(mine_hbm, mine_ref), (other_hbm, other_ref)], sem)
-    for head in range(GROUP):
-        sum_ref[head, :HD] = acc_ref[head].astype(jnp.float32)
-        sum_ref[head, HD:] = jnp.broadcast_to(
-            stat_ref[1, head : head + 1, :], (AUG - HD, sum_ref.shape[2])
-        )
-    wait_all(load)
+    first = 0
+    for stat_part, acc_part in ((stat_a_ref, acc_a_ref), (stat_b_ref, acc_b_ref)):
+        heads = acc_part.shape[0]
+        stat_ref[:, first : first + heads] = stat_part[...]
+        for head in range(heads):
+            sum_ref[first + head, :HD] = acc_part[head].astype(jnp.float32)
+            total = stat_part[1, head : head + 1, :]
+            sum_ref[first + head, HD:] = jnp.broadcast_to(total, (AUG - HD, sum_ref.shape[2]))
+        first += heads
     host = at_ref[0]
     chip, core = lax.div(host, 2), lax.rem(host, 2)
     senders, kept_rows, _ = mine_ref.shape
@@ -208,8 +210,11 @@
 
     @pl.when(jnp.logical_not(safe))
     def careful():
+        own_ref[:OWN_FIRST] = acc_a_ref[...]
+        own_ref[OWN_FIRST:] = acc_b_ref[...]
+
         def head_step(head, carry):
-            top, acc = careful_rows(q_ref, kv_ref, vt_ref, stat_ref, acc_ref, head, count)
+            top, acc = careful_rows(q_ref, kv_ref, vt_ref, stat_ref, own_ref, head, count)
             new_stat_ref[0, pl.ds(head, 1), :] = top
             new_stat_ref[1, pl.ds(head, 1), :] = acc[HD : HD + 1]
             new_acc_ref[head] = acc[:HD].astype(jnp.bfloat16)
@@ -284,6 +289,19 @@
     barrier = lax.optimization_barrier
 
     dma = pltpu.SemaphoreType.DMA
+
+    def own(first, count, weight, queries, own_kv):
+        return call(
+            functools.partial(own_kernel, first, count),
+            "own",
+            [VMEM] * 2,
+            [((2, count, tok), f32), ((count, HD, tok), bf16)],
+            (queries, own_kv),
+            [pltpu.VMEM((AUG, tok), bf16)],
+            flops=weight * GROUP * tok * tok * HD,
+            nbytes=1 << 10,
+        )
+
     with jax.named_scope("gather_hidden"):
         (hidden,) = call(
             repeat_kernel,
@@ -291,7 +309,7 @@
             [HBM],
             [((heads, *anchor_hidden.shape), bf16)],
             (anchor_hidden,),
-            [pltpu.VMEM(anchor_hidden.shape, bf16), dma((1,)), dma((heads,))],
+            [pltpu.VMEM(anchor_hidden.shape, bf16), dma((2,)), dma((2, heads))],
             nbytes=1 << 20,
             limit=63,
             out_spec=HBM,
@@ -318,54 +336,46 @@
         )
         kept, own_kv, queries = barrier((kept, own_kv, queries))
         row = [kept] + [lax.ppermute(kept, "hst", moves(0, d)) for d in range(1, SIDE)]
-
-    with jax.named_scope("own"):
-        stat, acc = call(
-            own_kernel,
-            "own",
-            [VMEM, VMEM],
-            state,
-            (queries, own_kv),
-            [pltpu.VMEM((AUG, tok), bf16)],
-            nbytes=1 << 10,
-        )
-    with jax.named_scope("kept_rows"):
-        *row, stat, acc = barrier((*row, stat, acc))
+        own_a = own(0, OWN_FIRST, 0, queries, own_kv)
+        *row, stat_a, acc_a = barrier((*row, *own_a))
         row = jnp.stack(row)
         plane = [row] + [lax.ppermute(row, "hst", moves(d, 0)) for d in range(1, SIDE)]
     with jax.named_scope("project"):
-        hidden, row, stat, acc = barrier((hidden, row, stat, acc))
+        hidden, row = barrier((hidden, row))
         (part,) = call(
             project_kernel,
             "project",
             [VMEM] * 2,
-            [((hosts, heads * rows, width), bf16)],
+            [((heads * rows, width), bf16)],
             (hidden, w_kv),
-            [pltpu.VMEM((heads * rows, width), bf16), dma((hosts,))],
             flops=2 * heads * rows * w_kv.shape[0] * width,
             nbytes=5 << 20,
-            out_spec=HBM,
-        )
-        _, *plane = barrier((part, *plane))
-        anchor = lax.all_to_all(part, "hst", 0, 0).reshape(hosts * heads * rows, width)
+        )
+        part = jnp.concatenate([part, lax.ppermute(part, "hst", moves(0, 0, 1))])
+        part = jnp.broadcast_to(part[None], (hosts // 2, *part.shape))
+        _, own_kv, queries, *plane = barrier((part, own_kv, queries, *plane))
+        same_core = [[2 * chip + core for chip in range(hosts // 2)] for core in range(2)]
+        anchor = lax.all_to_all(part, "hst", 0, 0, axis_index_groups=same_core)
+        anchor = anchor.reshape(hosts * heads * rows, width)
         mine = jnp.concatenate(plane)
         other = lax.ppermute(mine, "hst", moves(0, 0, 1))
+    with jax.named_scope("own"):
+        stat_b, acc_b = own(OWN_FIRST, GROUP - OWN_FIRST, 320, queries, own_kv)
     with jax.named_scope("kept"):
         stat, acc = call(
             kept_kernel,
             "kept",
-            [SMEM, VMEM, HBM, HBM, VMEM, VMEM],
+            [SMEM] + [VMEM] * 7,
             state,
-            (host[None].astype(jnp.int32), queries, mine, other, stat, acc),
+            (host[None].astype(jnp.int32), queries, mine, other, stat_a, acc_a, stat_b, acc_b),
             [
-                pltpu.VMEM(mine.shape, bf16),
-                pltpu.VMEM(mine.shape, bf16),
+                *(pltpu.VMEM(*one) for one in state),
                 pltpu.VMEM((GROUP, AUG, tok), f32),
                 pltpu.VMEM((hosts * kept_rows, width), bf16),
                 pltpu.VMEM((AUG, hosts * kept_rows), bf16),
-                dma((2,)),
             ],
-            nbytes=1 << 10,
+            flops=4 * GROUP * tok * hosts * kept_rows * HD,
+            nbytes=8 << 20,
         )
     with jax.named_scope("anchor"):
         (out,) = call(

time: 108 us -> 107 us (level)
  waiting for transfers between devices: 2.57 us -> 4.24 us
  Pallas kernels: 73.6 us -> 72 us
  local copies, waits for them, and re-layouts: 7.47 us -> 6.15 us
    unnamed x19 -> x17, local copies, waits for them, and re-layouts: 7.46 us -> 5.28 us
    pallas_call x6 -> x7, Pallas kernels: 73.6 us -> 72 us  [call(): pl.pallas_call(kernel, in_specs=in_specs, out_specs=[out_spec] * len(outs...]
  transfers between devices with their start and end apart: 9 -> 10, of which waited for: 1 -> 3; matrix products, arithmetic and copies ran while one was open for 1% -> 2% of each run, Pallas kernels for 46% -> 45%
where the time goes in v3:
time: 107 us; the launch traced here: 106 us
  Pallas kernels  72 us (67%)
  starting transfers between devices  23 us (21%)
  local copies, waits for them, and re-layouts  6.15 us (6%)
  waiting for transfers between devices  4.24 us (4%)
    pallas_call x7, Pallas kernels, call(): pl.pallas_call(kernel, in_specs=in_specs, out_specs=[out_spec] * len(outs...  72 us
    all_to_all x1, starting transfers between devices, per_device(): hidden = lax.all_to_all(hidden, 'tensor', 0, 0)  8.2 us
    all_to_all x1, starting transfers between devices, per_device(): anchor = lax.all_to_all(part, 'hst', 0, 0, axis_index_groups=same_core)  6.72 us
    unnamed x17, local copies, waits for them, and re-layouts  5.28 us
    ppermute x3, starting transfers between devices, per_device(): lax.ppermute(kept, 'hst', moves(0, d))  3.69 us
    all_to_all x1, waiting for transfers between devices, per_device(): hidden = lax.all_to_all(hidden, 'tensor', 0, 0)  2.99 us
    ppermute x3, starting transfers between devices, per_device(): lax.ppermute(row, 'hst', moves(d, 0))  2.87 us
  transfers between devices with their start and end apart: 10, of which 3 were waited for; matrix products, arithmetic and copies ran while one was open for 2% of the time, Pallas kernels for 45%

profile of v3, /device:TPU:17, one launch (start us, length us, event | category | flops | bytes accessed | tf_op | source)
XLA Modules:
  0.0 106.4 jit_solution(17718554619565379066)
XLA Ops:
  0.0 1.7 %repeat.1 = bf16[8,4,8192]{2,1,0:T(4,128)(2,1)} custom-call(bf16[4,8192]{1,0:T(4,128)(2,1)} %rows_hbm.1), custom_call_target="tpu_custom_call" | custom-call | bytes 1048576 | tf_op jit(solution)/shard_map/gather_hidden/repeat/pallas_call | solution.py:258
  1.7 8.2 %all-to-all-start = ((bf16[8,4,8192]{2,1,0:T(4,128)(2,1)}), bf16[8,4,8192]{2,1,0:T(4,128)(2,1)S(1)}, u32[]{:S(2)}, u32[]{:S(2)}) async-start(bf16[8,4,8192]{2,1,0:T(4,128)(2,1)} %repeat.1), calls=%async_computation | async-start | bytes 1048576 | tf_op jit(solution)/shard_map/gather_hidden/all_to_all | solution.py:318
  9.9 1.8 %select.1 = bf16[64,256]{1,0:T(8,128)(2,1)} custom-call(s32[1,64]{1,0:T(1,128)} %bitcast.12, bf16[512,256]{1,0:T(8,128)(2,1)} %kv_ref.1), custom_call_target="tpu_custom_call" | custom-call | flops 16777216 | bytes 262144 | tf_op jit(solution)/shard_map/select_kept/select/pallas_call | solution.py:258
  11.7 2.6 %collective-permute-start.2 = (bf16[64,256]{1,0:T(8,128)(2,1)}, bf16[64,256]{1,0:T(8,128)(2,1)S(1)}, u32[]{:S(2)}, u32[]{:S(2)}) collective-permute-start(bf16[64,256]{1,0:T(8,128)(2,1)} %select.1), channel_id=1, source_target_pairs={{0,48},{8,56},{16,0},{24,8},{32,16},{40,24},{48,32},{56,40},{64,11... | collective-permute-start | bytes 98312 | tf_op jit(solution)/shard_map/select_kept/ppermute | solution.py:338
  14.3 0.5 collective-permute-start.1
  14.8 0.6 collective-permute-start
  15.4 1.2 %copy-done = bf16[512,1024]{1,0:T(8,128)(2,1)S(1)} copy-done((bf16[512,1024]{1,0:T(8,128)(2,1)S(1)}, bf16[512,1024]{1,0:T(8,128)(2,1)}, u32[]{:S(2)}) %copy-start) | copy-done | bytes 1048600
  16.6 0.9 copy-done.3
  17.6 2.7 %own.2 = (f32[2,6,512]{2,1,0:T(8,128)S(1)}, bf16[6,128,512]{2,1,0:T(8,128)(2,1)S(1)}) custom-call(bf16[512,1024]{1,0:T(8,128)(2,1)S(1)} %copy-done, bf16[512,256]{1,0:T(8,128)(2,1)S(1)} %copy-done.3), custom_call_target="tpu_custom_call" | custom-call | bytes 1024 | tf_op jit(solution)/shard_map/select_kept/own/pallas_call | solution.py:258
  20.3 0.0 copy-start.5
  20.3 0.9 copy-done.5
  21.1 0.0 collective-permute-done.2
  21.1 0.0 collective-permute-done.1
  21.2 0.0 collective-permute-done
  21.2 0.9 pad_maximum_fusion
  22.0 0.2 collective-permute-start.6
  22.3 2.6 %collective-permute-start.5 = (bf16[4,64,256]{2,1,0:T(8,128)(2,1)S(1)}, bf16[4,64,256]{2,1,0:T(8,128)(2,1)S(1)}, u32[]{:S(2)}, u32[]{:S(2)}) collective-permute-start(bf16[4,64,256]{2,1,0:T(8,128)(2,1)S(1)} %pad_maximum_fusion), channel_id=1, source_target_pairs={{0,128},{8,136},{16,144},{24,152},{32,160},{40,168},{48,176},{56,1... | collective-permute-start | bytes 393224 | tf_op jit(solution)/shard_map/select_kept/ppermute | solution.py:342
  24.9 0.0 collective-permute-start.4
  24.9 3.0 %all-to-all-done.rows_ref = bf16[8,4,8192]{2,1,0:T(4,128)(2,1)S(1)} async-done(((bf16[8,4,8192]{2,1,0:T(4,128)(2,1)}), bf16[8,4,8192]{2,1,0:T(4,128)(2,1)S(1)}, u32[]{:S(2)}, u32[]{:S(2)}) %all-to-all-start) | async-done | bytes 524320 | tf_op jit(solution)/shard_map/gather_hidden/all_to_all | solution.py:318
  27.9 2.2 %copy-done.2 = bf16[8192,256]{1,0:T(8,128)(2,1)S(1)} copy-done((bf16[8192,256]{1,0:T(8,128)(2,1)S(1)}, bf16[8192,256]{1,0:T(8,128)(2,1)}, u32[]{:S(2)}) %copy-start.2) | copy-done | bytes 4194328
  30.1 0.8 project.1
  30.9 0.5 collective-permute-start.3
  31.4 0.8 collective-permute-done.3
  32.2 0.9 broadcast_in_dim.4
  33.1 6.7 %all-to-all-start.1 = ((bf16[16,64,256]{2,1,0:T(8,128)(2,1)}), bf16[16,64,256]{2,1,0:T(8,128)(2,1)S(1)}, u32[]{:S(2)}, u32[]{:S(2)}) async-start(bf16[16,64,256]{2,1,0:T(8,128)(2,1)} %broadcast_in_dim.4), calls=%async_computation.1 | async-start | bytes 1048576 | tf_op jit(solution)/shard_map/project/all_to_all | solution.py:358
  39.8 0.0 collective-permute-done.6
  39.9 0.0 copy-start.6
  39.9 1.0 collective-permute-start.7
  40.9 1.1 %own.3 = (f32[2,2,512]{2,1,0:T(2,128)S(1)}, bf16[2,128,512]{2,1,0:T(8,128)(2,1)S(1)}) custom-call(bf16[512,1024]{1,0:T(8,128)(2,1)S(1)} %copy-done.1, bf16[512,256]{1,0:T(8,128)(2,1)S(1)} %copy-done.4), custom_call_target="tpu_custom_call" | custom-call | flops 85899345920 | bytes 1024 | tf_op jit(solution)/shard_map/own/own/pallas_call | solution.py:258
  42.1 0.4 collective-permute-done.7.other_ref
  42.5 41.6 %kept.1 = (f32[2,8,512]{2,1,0:T(8,128)S(1)}, bf16[8,128,512]{2,1,0:T(8,128)(2,1)S(1)}) custom-call(s32[1]{0:T(128)} %bitcast.6.at_ref, bf16[512,1024]{1,0:T(8,128)(2,1)S(1)} %copy-done.1, bf16[16,64,256]{2,1,0:T(8,128)(2,1)S(1)} %constant_dynamic-update-slice_fusion.mine_ref, bf16[16,64,256]{2,1,0:T(8,128)(2,1)S(1)} %collective-permute-done.7.other_ref, ...), custom_call_target="tpu_custom_call" | custom-call | flops 4294967296 | bytes 8388608 | tf_op jit(solution)/shard_map/kept/kept/pallas_call | solution.py:258
  84.0 22.3 %anchor.1 = bf16[512,1024]{1,0:T(8,128)(2,1)} custom-call(bf16[512,1024]{1,0:T(8,128)(2,1)S(1)} %copy-done.1, bf16[1024,256]{1,0:T(8,128)(2,1)S(1)} %bitcast.7, f32[2,8,512]{2,1,0:T(8,128)S(1)} %get-tuple-element.55.stat_ref, bf16[8,128,512]{2,1,0:T(8,128)(2,1)S(1)} %get-tuple-element.56.acc_ref), custom_call_target="tpu_custom_call" | custom-call | bytes 1048576 | tf_op jit(solution)/shard_map/anchor/anchor/pallas_call | solution.py:258
  (16 shorter events, 0.1 us)
Async XLA Ops:
  1.7 26.2 %all-to-all-start = ((bf16[8,4,8192]{2,1,0:T(4,128)(2,1)}), bf16[8,4,8192]{2,1,0:T(4,128)(2,1)S(1)}, u32[]{:S(2)}, u32[]{:S(2)}) async-start(bf16[8,4,8192]{2,1,0:T(4,128)(2,1)} %repeat.1), calls=%async_computation | async-start | bytes 1048576 | tf_op jit(solution)/shard_map/gather_hidden/all_to_all | solution.py:318
  11.7 9.4 %collective-permute-start.2 = (bf16[64,256]{1,0:T(8,128)(2,1)}, bf16[64,256]{1,0:T(8,128)(2,1)S(1)}, u32[]{:S(2)}, u32[]{:S(2)}) collective-permute-start(bf16[64,256]{1,0:T(8,128)(2,1)} %select.1), channel_id=1, source_target_pairs={{0,48},{8,56},{16,0},{24,8},{32,16},{40,24},{48,32},{56,40},{64,11... | collective-permute-start | bytes 98312 | tf_op jit(solution)/shard_map/select_kept/ppermute | solution.py:338
  14.3 6.9 %collective-permute-start.1 = (bf16[64,256]{1,0:T(8,128)(2,1)}, bf16[64,256]{1,0:T(8,128)(2,1)S(1)}, u32[]{:S(2)}, u32[]{:S(2)}) collective-permute-start(bf16[64,256]{1,0:T(8,128)(2,1)} %select.1), channel_id=1, source_target_pairs={{0,32},{8,40},{16,48},{24,56},{32,0},{40,8},{48,16},{56,24},{64,96... | collective-permute-start | bytes 98312 | tf_op jit(solution)/shard_map/select_kept/ppermute | solution.py:338
  14.8 6.4 %collective-permute-start = (bf16[64,256]{1,0:T(8,128)(2,1)}, bf16[64,256]{1,0:T(8,128)(2,1)S(1)}, u32[]{:S(2)}, u32[]{:S(2)}) collective-permute-start(bf16[64,256]{1,0:T(8,128)(2,1)} %select.1), channel_id=1, source_target_pairs={{0,16},{8,24},{16,32},{24,40},{32,48},{40,56},{48,0},{56,8},{64,80... | collective-permute-start | bytes 98312 | tf_op jit(solution)/shard_map/select_kept/ppermute | solution.py:338
  15.4 1.2 %copy-start = (bf16[512,1024]{1,0:T(8,128)(2,1)S(1)}, bf16[512,1024]{1,0:T(8,128)(2,1)}, u32[]{:S(2)}) copy-start(bf16[512,1024]{1,0:T(8,128)(2,1)} %q_ref.3) | copy-start | bytes 3145732
  16.6 0.9 copy-start.3
  17.6 23.4 %copy-start.4 = (bf16[512,256]{1,0:T(8,128)(2,1)S(1)}, bf16[512,256]{1,0:T(8,128)(2,1)}, u32[]{:S(2)}) copy-start(bf16[512,256]{1,0:T(8,128)(2,1)} %kv_ref.1) | copy-start | bytes 786436
  20.3 0.9 copy-start.5
  21.1 19.8 %copy-start.1 = (bf16[512,1024]{1,0:T(8,128)(2,1)S(1)}, bf16[512,1024]{1,0:T(8,128)(2,1)}, u32[]{:S(2)}) copy-start(bf16[512,1024]{1,0:T(8,128)(2,1)} %q_ref.3) | copy-start | bytes 3145732
  22.0 17.8 %collective-permute-start.6 = (bf16[4,64,256]{2,1,0:T(8,128)(2,1)S(1)}, bf16[4,64,256]{2,1,0:T(8,128)(2,1)S(1)}, u32[]{:S(2)}, u32[]{:S(2)}) collective-permute-start(bf16[4,64,256]{2,1,0:T(8,128)(2,1)S(1)} %pad_maximum_fusion), channel_id=1, source_target_pairs={{0,192},{8,200},{16,208},{24,216},{32,224},{40,232},{48,240},{56,2... | collective-permute-start | bytes 393224 | tf_op jit(solution)/shard_map/select_kept/ppermute | solution.py:342
  22.3 17.6 %collective-permute-start.5 = (bf16[4,64,256]{2,1,0:T(8,128)(2,1)S(1)}, bf16[4,64,256]{2,1,0:T(8,128)(2,1)S(1)}, u32[]{:S(2)}, u32[]{:S(2)}) collective-permute-start(bf16[4,64,256]{2,1,0:T(8,128)(2,1)S(1)} %pad_maximum_fusion), channel_id=1, source_target_pairs={{0,128},{8,136},{16,144},{24,152},{32,160},{40,168},{48,176},{56,1... | collective-permute-start | bytes 393224 | tf_op jit(solution)/shard_map/select_kept/ppermute | solution.py:342
  24.9 14.9 %collective-permute-start.4 = (bf16[4,64,256]{2,1,0:T(8,128)(2,1)S(1)}, bf16[4,64,256]{2,1,0:T(8,128)(2,1)S(1)}, u32[]{:S(2)}, u32[]{:S(2)}) collective-permute-start(bf16[4,64,256]{2,1,0:T(8,128)(2,1)S(1)} %pad_maximum_fusion), channel_id=1, source_target_pairs={{0,64},{8,72},{16,80},{24,88},{32,96},{40,104},{48,112},{56,120},{... | collective-permute-start | bytes 393224 | tf_op jit(solution)/shard_map/select_kept/ppermute | solution.py:342
  27.9 2.2 %copy-start.2 = (bf16[8192,256]{1,0:T(8,128)(2,1)S(1)}, bf16[8192,256]{1,0:T(8,128)(2,1)}, u32[]{:S(2)}) copy-start(bf16[8192,256]{1,0:T(8,128)(2,1)} %w_ref.1) | copy-start | bytes 12582916
  30.9 1.3 %collective-permute-start.3 = (bf16[32,256]{1,0:T(8,128)(2,1)S(1)}, bf16[32,256]{1,0:T(8,128)(2,1)S(1)}, u32[]{:S(2)}, u32[]{:S(2)}) collective-permute-start(bf16[32,256]{1,0:T(8,128)(2,1)S(1)} %project.1), channel_id=1, source_target_pairs={{0,8},{8,0},{16,24},{24,16},{32,40},{40,32},{48,56},{56,48},{64,72... | collective-permute-start | bytes 49160 | tf_op jit(solution)/shard_map/project/ppermute | solution.py:354
  33.1 50.9 %all-to-all-start.1 = ((bf16[16,64,256]{2,1,0:T(8,128)(2,1)}), bf16[16,64,256]{2,1,0:T(8,128)(2,1)S(1)}, u32[]{:S(2)}, u32[]{:S(2)}) async-start(bf16[16,64,256]{2,1,0:T(8,128)(2,1)} %broadcast_in_dim.4), calls=%async_computation.1 | async-start | bytes 1048576 | tf_op jit(solution)/shard_map/project/all_to_all | solution.py:358
  39.9 2.5 %copy-start.6 = (bf16[6,128,512]{2,1,0:T(8,128)(2,1)S(1)}, bf16[6,128,512]{2,1,0:T(8,128)(2,1)}, u32[]{:S(2)}) copy-start(bf16[6,128,512]{2,1,0:T(8,128)(2,1)} %copy-done.5) | copy-start | bytes 2359300
  39.9 2.5 %collective-permute-start.7 = (bf16[16,64,256]{2,1,0:T(8,128)(2,1)S(1)}, bf16[16,64,256]{2,1,0:T(8,128)(2,1)S(1)}, u32[]{:S(2)}, u32[]{:S(2)}) collective-permute-start(bf16[16,64,256]{2,1,0:T(8,128)(2,1)S(1)} %constant_dynamic-update-slice_fusion.mine_ref), channel_id=1, source_target_pairs={{0,8},{8,0},{16,24},{24,16},{32,40},{40,32},{48,56},{56,48},{64,72... | collective-permute-start | bytes 1572872 | tf_op jit(solution)/shard_map/project/ppermute | solution.py:361

commit v4 on v3

--- a/solution.py
+++ b/solution.py
@@ -17,7 +17,7 @@
 KEPT_BLOCK = 1024
 SIDE = 4
 OWN_FIRST = 6
-HEAD_STEP = 4
+HEAD_STEP = 8
 SAFE_TOTAL = 2.0**100
 
 
@@ -223,18 +223,27 @@
         lax.fori_loop(0, GROUP, head_step, 0)
 
 
-def anchor_kernel(q_ref, kv_ref, stat_ref, acc_ref, out_ref, vt_ref, total_ref):
+def anchor_kernel(
+    q_ref, kv_ref, stat_ref, acc_ref, out_hbm, out_ref, vt_ref, total_ref, sem
+):
     fill_values(vt_ref, kv_ref)
     rows = kv_ref.shape[0]
 
+    def store(head):
+        return pltpu.make_async_copy(
+            out_ref.at[head], out_hbm.at[:, head_cols(head)], sem.at[head]
+        )
+
     def finish(head, acc, total):
-        out_ref[:, head_cols(head)] = (acc * (1.0 / total)).T.astype(jnp.bfloat16)
+        out_ref[head] = (acc * (1.0 / total)).T.astype(jnp.bfloat16)
+        store(head).start()
 
     for head in range(GROUP):
         term = fast_rows(q_ref, kv_ref, vt_ref, stat_ref, head, 0, rows)
         total = stat_ref[1, head : head + 1, :] + term[HD : HD + 1]
         total_ref[head : head + 1, :] = total
         finish(head, acc_ref[head].astype(jnp.float32) + term[:HD], total)
+    wait_all([store(head) for head in range(GROUP)])
     safe = jnp.all(total_ref[...] < SAFE_TOTAL)
 
     @pl.when(jnp.logical_not(safe))
@@ -242,6 +251,7 @@
         def head_step(head, carry):
             _, acc = careful_rows(q_ref, kv_ref, vt_ref, stat_ref, acc_ref, head, rows)
             finish(head, acc[:HD], acc[HD : HD + 1])
+            store(head).wait()
             return carry
 
         lax.fori_loop(0, GROUP, head_step, 0)
@@ -384,7 +394,13 @@
             [VMEM] * 4,
             [((tok, GROUP * HD), bf16)],
             (queries, anchor, stat, acc),
-            [pltpu.VMEM((AUG, anchor.shape[0]), bf16), pltpu.VMEM((GROUP, tok), f32)],
+            [
+                pltpu.VMEM((GROUP, tok, HD), bf16),
+                pltpu.VMEM((AUG, anchor.shape[0]), bf16),
+                pltpu.VMEM((GROUP, tok), f32),
+                dma((GROUP,)),
+            ],
+            out_spec=HBM,
             nbytes=1 << 20,
         )
     return out

time: 107 us -> 112 us (1.047)
  Pallas kernels: 72 us -> 77.1 us
    pallas_call x7, Pallas kernels: 72 us -> 77.1 us  [call(): pl.pallas_call(kernel, in_specs=in_specs, out_specs=[out_spec] * len(outs...]
  transfers between devices with their start and end apart: 10 -> 10, of which waited for: 3 -> 3; matrix products, arithmetic and copies ran while one was open for 2% -> 2% of each run, Pallas kernels for 45% -> 43%
where the time goes in v4:
time: 112 us
  Pallas kernels  77.1 us (69%)
  starting transfers between devices  23 us (21%)
  local copies, waits for them, and re-layouts  6.15 us (5%)
  waiting for transfers between devices  4.24 us (4%)
    pallas_call x7, Pallas kernels, call(): pl.pallas_call(kernel, in_specs=in_specs, out_specs=[out_spec] * len(outs...  77.1 us
    all_to_all x1, starting transfers between devices, per_device(): hidden = lax.all_to_all(hidden, 'tensor', 0, 0)  8.2 us
    all_to_all x1, starting transfers between devices, per_device(): anchor = lax.all_to_all(part, 'hst', 0, 0, axis_index_groups=same_core)  6.72 us
    unnamed x17, local copies, waits for them, and re-layouts  5.28 us
    ppermute x3, starting transfers between devices, per_device(): lax.ppermute(kept, 'hst', moves(0, d))  3.69 us
    all_to_all x1, waiting for transfers between devices, per_device(): hidden = lax.all_to_all(hidden, 'tensor', 0, 0)  2.99 us
    ppermute x3, starting transfers between devices, per_device(): lax.ppermute(row, 'hst', moves(d, 0))  2.87 us
  transfers between devices with their start and end apart: 10, of which 3 were waited for; matrix products, arithmetic and copies ran while one was open for 2% of the time, Pallas kernels for 43%

profile of v4, /device:TPU:17, one launch (start us, length us, event | category | flops | bytes accessed | tf_op | source)
XLA Modules:
  0.0 111.6 jit_solution(15669110509091625904)
XLA Ops:
  0.0 1.7 %repeat.1 = bf16[8,4,8192]{2,1,0:T(4,128)(2,1)} custom-call(bf16[4,8192]{1,0:T(4,128)(2,1)} %rows_hbm.1), custom_call_target="tpu_custom_call" | custom-call | bytes 1048576 | tf_op jit(solution)/shard_map/gather_hidden/repeat/pallas_call | solution.py:268
  1.7 8.2 %all-to-all-start = ((bf16[8,4,8192]{2,1,0:T(4,128)(2,1)}), bf16[8,4,8192]{2,1,0:T(4,128)(2,1)S(1)}, u32[]{:S(2)}, u32[]{:S(2)}) async-start(bf16[8,4,8192]{2,1,0:T(4,128)(2,1)} %repeat.1), calls=%async_computation | async-start | bytes 1048576 | tf_op jit(solution)/shard_map/gather_hidden/all_to_all | solution.py:328
  9.9 1.8 %select.1 = bf16[64,256]{1,0:T(8,128)(2,1)} custom-call(s32[1,64]{1,0:T(1,128)} %bitcast.12, bf16[512,256]{1,0:T(8,128)(2,1)} %kv_ref.1), custom_call_target="tpu_custom_call" | custom-call | flops 16777216 | bytes 262144 | tf_op jit(solution)/shard_map/select_kept/select/pallas_call | solution.py:268
  11.7 2.6 %collective-permute-start.2 = (bf16[64,256]{1,0:T(8,128)(2,1)}, bf16[64,256]{1,0:T(8,128)(2,1)S(1)}, u32[]{:S(2)}, u32[]{:S(2)}) collective-permute-start(bf16[64,256]{1,0:T(8,128)(2,1)} %select.1), channel_id=1, source_target_pairs={{0,48},{8,56},{16,0},{24,8},{32,16},{40,24},{48,32},{56,40},{64,11... | collective-permute-start | bytes 98312 | tf_op jit(solution)/shard_map/select_kept/ppermute | solution.py:348
  14.3 0.5 collective-permute-start.1
  14.8 0.6 collective-permute-start
  15.4 1.2 %copy-done = bf16[512,1024]{1,0:T(8,128)(2,1)S(1)} copy-done((bf16[512,1024]{1,0:T(8,128)(2,1)S(1)}, bf16[512,1024]{1,0:T(8,128)(2,1)}, u32[]{:S(2)}) %copy-start) | copy-done | bytes 1048600
  16.6 0.9 copy-done.3
  17.6 2.7 %own.2 = (f32[2,6,512]{2,1,0:T(8,128)S(1)}, bf16[6,128,512]{2,1,0:T(8,128)(2,1)S(1)}) custom-call(bf16[512,1024]{1,0:T(8,128)(2,1)S(1)} %copy-done, bf16[512,256]{1,0:T(8,128)(2,1)S(1)} %copy-done.3), custom_call_target="tpu_custom_call" | custom-call | bytes 1024 | tf_op jit(solution)/shard_map/select_kept/own/pallas_call | solution.py:268
  20.3 0.0 copy-start.5
  20.3 0.9 copy-done.5
  21.1 0.0 collective-permute-done.2
  21.1 0.0 collective-permute-done.1
  21.2 0.0 collective-permute-done
  21.2 0.9 pad_maximum_fusion
  22.0 0.2 collective-permute-start.6
  22.3 2.6 %collective-permute-start.5 = (bf16[4,64,256]{2,1,0:T(8,128)(2,1)S(1)}, bf16[4,64,256]{2,1,0:T(8,128)(2,1)S(1)}, u32[]{:S(2)}, u32[]{:S(2)}) collective-permute-start(bf16[4,64,256]{2,1,0:T(8,128)(2,1)S(1)} %pad_maximum_fusion), channel_id=1, source_target_pairs={{0,128},{8,136},{16,144},{24,152},{32,160},{40,168},{48,176},{56,1... | collective-permute-start | bytes 393224 | tf_op jit(solution)/shard_map/select_kept/ppermute | solution.py:352
  24.9 0.0 collective-permute-start.4
  24.9 3.0 %all-to-all-done.rows_ref = bf16[8,4,8192]{2,1,0:T(4,128)(2,1)S(1)} async-done(((bf16[8,4,8192]{2,1,0:T(4,128)(2,1)}), bf16[8,4,8192]{2,1,0:T(4,128)(2,1)S(1)}, u32[]{:S(2)}, u32[]{:S(2)}) %all-to-all-start) | async-done | bytes 524320 | tf_op jit(solution)/shard_map/gather_hidden/all_to_all | solution.py:328
  27.9 2.2 %copy-done.2 = bf16[8192,256]{1,0:T(8,128)(2,1)S(1)} copy-done((bf16[8192,256]{1,0:T(8,128)(2,1)S(1)}, bf16[8192,256]{1,0:T(8,128)(2,1)}, u32[]{:S(2)}) %copy-start.2) | copy-done | bytes 4194328
  30.1 0.8 project.1
  30.9 0.5 collective-permute-start.3
  31.4 0.8 collective-permute-done.3
  32.2 0.9 broadcast_in_dim.4
  33.1 6.7 %all-to-all-start.1 = ((bf16[16,64,256]{2,1,0:T(8,128)(2,1)}), bf16[16,64,256]{2,1,0:T(8,128)(2,1)S(1)}, u32[]{:S(2)}, u32[]{:S(2)}) async-start(bf16[16,64,256]{2,1,0:T(8,128)(2,1)} %broadcast_in_dim.4), calls=%async_computation.1 | async-start | bytes 1048576 | tf_op jit(solution)/shard_map/project/all_to_all | solution.py:368
  39.8 0.0 collective-permute-done.5
  39.9 0.0 copy-start.6
  39.9 1.0 collective-permute-start.7
  40.9 1.1 %own.3 = (f32[2,2,512]{2,1,0:T(2,128)S(1)}, bf16[2,128,512]{2,1,0:T(8,128)(2,1)S(1)}) custom-call(bf16[512,1024]{1,0:T(8,128)(2,1)S(1)} %copy-done.1, bf16[512,256]{1,0:T(8,128)(2,1)S(1)} %copy-done.4), custom_call_target="tpu_custom_call" | custom-call | flops 85899345920 | bytes 1024 | tf_op jit(solution)/shard_map/own/own/pallas_call | solution.py:268
  42.1 0.4 collective-permute-done.7.other_ref
  42.5 41.7 %kept.1 = (f32[2,8,512]{2,1,0:T(8,128)S(1)}, bf16[8,128,512]{2,1,0:T(8,128)(2,1)S(1)}) custom-call(s32[1]{0:T(128)} %bitcast.6.at_ref, bf16[512,1024]{1,0:T(8,128)(2,1)S(1)} %copy-done.1, bf16[16,64,256]{2,1,0:T(8,128)(2,1)S(1)} %constant_dynamic-update-slice_fusion.mine_ref, bf16[16,64,256]{2,1,0:T(8,128)(2,1)S(1)} %collective-permute-done.7.other_ref, ...), custom_call_target="tpu_custom_call" | custom-call | flops 4294967296 | bytes 8388608 | tf_op jit(solution)/shard_map/kept/kept/pallas_call | solution.py:268
  84.2 27.3 %anchor.1 = bf16[512,1024]{1,0:T(8,128)(2,1)} custom-call(bf16[512,1024]{1,0:T(8,128)(2,1)S(1)} %copy-done.1, bf16[1024,256]{1,0:T(8,128)(2,1)S(1)} %bitcast.7, f32[2,8,512]{2,1,0:T(8,128)S(1)} %get-tuple-element.55.stat_ref, bf16[8,128,512]{2,1,0:T(8,128)(2,1)S(1)} %get-tuple-element.56.acc_ref), custom_call_target="tpu_custom_call" | custom-call | bytes 1048576 | tf_op jit(solution)/shard_map/anchor/anchor/pallas_call | solution.py:268
  (16 shorter events, 0.1 us)
Async XLA Ops:
  1.7 26.2 %all-to-all-start = ((bf16[8,4,8192]{2,1,0:T(4,128)(2,1)}), bf16[8,4,8192]{2,1,0:T(4,128)(2,1)S(1)}, u32[]{:S(2)}, u32[]{:S(2)}) async-start(bf16[8,4,8192]{2,1,0:T(4,128)(2,1)} %repeat.1), calls=%async_computation | async-start | bytes 1048576 | tf_op jit(solution)/shard_map/gather_hidden/all_to_all | solution.py:328
  11.7 9.4 %collective-permute-start.2 = (bf16[64,256]{1,0:T(8,128)(2,1)}, bf16[64,256]{1,0:T(8,128)(2,1)S(1)}, u32[]{:S(2)}, u32[]{:S(2)}) collective-permute-start(bf16[64,256]{1,0:T(8,128)(2,1)} %select.1), channel_id=1, source_target_pairs={{0,48},{8,56},{16,0},{24,8},{32,16},{40,24},{48,32},{56,40},{64,11... | collective-permute-start | bytes 98312 | tf_op jit(solution)/shard_map/select_kept/ppermute | solution.py:348
  14.3 6.9 %collective-permute-start.1 = (bf16[64,256]{1,0:T(8,128)(2,1)}, bf16[64,256]{1,0:T(8,128)(2,1)S(1)}, u32[]{:S(2)}, u32[]{:S(2)}) collective-permute-start(bf16[64,256]{1,0:T(8,128)(2,1)} %select.1), channel_id=1, source_target_pairs={{0,32},{8,40},{16,48},{24,56},{32,0},{40,8},{48,16},{56,24},{64,96... | collective-permute-start | bytes 98312 | tf_op jit(solution)/shard_map/select_kept/ppermute | solution.py:348
  14.8 6.4 %collective-permute-start = (bf16[64,256]{1,0:T(8,128)(2,1)}, bf16[64,256]{1,0:T(8,128)(2,1)S(1)}, u32[]{:S(2)}, u32[]{:S(2)}) collective-permute-start(bf16[64,256]{1,0:T(8,128)(2,1)} %select.1), channel_id=1, source_target_pairs={{0,16},{8,24},{16,32},{24,40},{32,48},{40,56},{48,0},{56,8},{64,80... | collective-permute-start | bytes 98312 | tf_op jit(solution)/shard_map/select_kept/ppermute | solution.py:348
  15.4 1.2 %copy-start = (bf16[512,1024]{1,0:T(8,128)(2,1)S(1)}, bf16[512,1024]{1,0:T(8,128)(2,1)}, u32[]{:S(2)}) copy-start(bf16[512,1024]{1,0:T(8,128)(2,1)} %q_ref.3) | copy-start | bytes 3145732
  16.6 0.9 copy-start.3
  17.6 23.4 %copy-start.4 = (bf16[512,256]{1,0:T(8,128)(2,1)S(1)}, bf16[512,256]{1,0:T(8,128)(2,1)}, u32[]{:S(2)}) copy-start(bf16[512,256]{1,0:T(8,128)(2,1)} %kv_ref.1) | copy-start | bytes 786436
  20.3 0.9 copy-start.5
  21.1 19.8 %copy-start.1 = (bf16[512,1024]{1,0:T(8,128)(2,1)S(1)}, bf16[512,1024]{1,0:T(8,128)(2,1)}, u32[]{:S(2)}) copy-start(bf16[512,1024]{1,0:T(8,128)(2,1)} %q_ref.3) | copy-start | bytes 3145732
  22.0 17.8 %collective-permute-start.6 = (bf16[4,64,256]{2,1,0:T(8,128)(2,1)S(1)}, bf16[4,64,256]{2,1,0:T(8,128)(2,1)S(1)}, u32[]{:S(2)}, u32[]{:S(2)}) collective-permute-start(bf16[4,64,256]{2,1,0:T(8,128)(2,1)S(1)} %pad_maximum_fusion), channel_id=1, source_target_pairs={{0,192},{8,200},{16,208},{24,216},{32,224},{40,232},{48,240},{56,2... | collective-permute-start | bytes 393224 | tf_op jit(solution)/shard_map/select_kept/ppermute | solution.py:352
  22.3 17.6 %collective-permute-start.5 = (bf16[4,64,256]{2,1,0:T(8,128)(2,1)S(1)}, bf16[4,64,256]{2,1,0:T(8,128)(2,1)S(1)}, u32[]{:S(2)}, u32[]{:S(2)}) collective-permute-start(bf16[4,64,256]{2,1,0:T(8,128)(2,1)S(1)} %pad_maximum_fusion), channel_id=1, source_target_pairs={{0,128},{8,136},{16,144},{24,152},{32,160},{40,168},{48,176},{56,1... | collective-permute-start | bytes 393224 | tf_op jit(solution)/shard_map/select_kept/ppermute | solution.py:352
  24.9 14.9 %collective-permute-start.4 = (bf16[4,64,256]{2,1,0:T(8,128)(2,1)S(1)}, bf16[4,64,256]{2,1,0:T(8,128)(2,1)S(1)}, u32[]{:S(2)}, u32[]{:S(2)}) collective-permute-start(bf16[4,64,256]{2,1,0:T(8,128)(2,1)S(1)} %pad_maximum_fusion), channel_id=1, source_target_pairs={{0,64},{8,72},{16,80},{24,88},{32,96},{40,104},{48,112},{56,120},{... | collective-permute-start | bytes 393224 | tf_op jit(solution)/shard_map/select_kept/ppermute | solution.py:352
  27.9 2.2 %copy-start.2 = (bf16[8192,256]{1,0:T(8,128)(2,1)S(1)}, bf16[8192,256]{1,0:T(8,128)(2,1)}, u32[]{:S(2)}) copy-start(bf16[8192,256]{1,0:T(8,128)(2,1)} %w_ref.1) | copy-start | bytes 12582916
  30.9 1.3 %collective-permute-start.3 = (bf16[32,256]{1,0:T(8,128)(2,1)S(1)}, bf16[32,256]{1,0:T(8,128)(2,1)S(1)}, u32[]{:S(2)}, u32[]{:S(2)}) collective-permute-start(bf16[32,256]{1,0:T(8,128)(2,1)S(1)} %project.1), channel_id=1, source_target_pairs={{0,8},{8,0},{16,24},{24,16},{32,40},{40,32},{48,56},{56,48},{64,72... | collective-permute-start | bytes 49160 | tf_op jit(solution)/shard_map/project/ppermute | solution.py:364
  33.1 51.1 %all-to-all-start.1 = ((bf16[16,64,256]{2,1,0:T(8,128)(2,1)}), bf16[16,64,256]{2,1,0:T(8,128)(2,1)S(1)}, u32[]{:S(2)}, u32[]{:S(2)}) async-start(bf16[16,64,256]{2,1,0:T(8,128)(2,1)} %broadcast_in_dim.4), calls=%async_computation.1 | async-start | bytes 1048576 | tf_op jit(solution)/shard_map/project/all_to_all | solution.py:368
  39.9 2.5 %copy-start.6 = (bf16[6,128,512]{2,1,0:T(8,128)(2,1)S(1)}, bf16[6,128,512]{2,1,0:T(8,128)(2,1)}, u32[]{:S(2)}) copy-start(bf16[6,128,512]{2,1,0:T(8,128)(2,1)} %copy-done.5) | copy-start | bytes 2359300
  39.9 2.5 %collective-permute-start.7 = (bf16[16,64,256]{2,1,0:T(8,128)(2,1)S(1)}, bf16[16,64,256]{2,1,0:T(8,128)(2,1)S(1)}, u32[]{:S(2)}, u32[]{:S(2)}) collective-permute-start(bf16[16,64,256]{2,1,0:T(8,128)(2,1)S(1)} %constant_dynamic-update-slice_fusion.mine_ref), channel_id=1, source_target_pairs={{0,8},{8,0},{16,24},{24,16},{32,40},{40,32},{48,56},{56,48},{64,72... | collective-permute-start | bytes 1572872 | tf_op jit(solution)/shard_map/project/ppermute | solution.py:371

commit v5 on v4

--- a/solution.py
+++ b/solution.py
@@ -16,7 +16,7 @@
 KEY_BLOCK = 256
 KEPT_BLOCK = 1024
 SIDE = 4
-OWN_FIRST = 6
+OWN_FIRST = 7
 HEAD_STEP = 8
 SAFE_TOTAL = 2.0**100
 
@@ -235,7 +235,7 @@
         )
 
     def finish(head, acc, total):
-        out_ref[head] = (acc * (1.0 / total)).T.astype(jnp.bfloat16)
+        out_ref[head] = (acc * (1.0 / total)).astype(jnp.bfloat16).T
         store(head).start()
 
     for head in range(GROUP):

time: 112 us -> 112 us (level)
  no operation moved by 1% of the time
where the time goes in v5:
time: 112 us
  Pallas kernels  77 us (69%)
  starting transfers between devices  23 us (21%)
  local copies, waits for them, and re-layouts  6.19 us (6%)
  waiting for transfers between devices  4.18 us (4%)
    pallas_call x7, Pallas kernels, call(): pl.pallas_call(kernel, in_specs=in_specs, out_specs=[out_spec] * len(outs...  77 us
    all_to_all x1, starting transfers between devices, per_device(): hidden = lax.all_to_all(hidden, 'tensor', 0, 0)  8.2 us
    all_to_all x1, starting transfers between devices, per_device(): anchor = lax.all_to_all(part, 'hst', 0, 0, axis_index_groups=same_core)  6.72 us
    unnamed x17, local copies, waits for them, and re-layouts  5.33 us
    ppermute x3, starting transfers between devices, per_device(): lax.ppermute(kept, 'hst', moves(0, d))  3.69 us
    ppermute x3, starting transfers between devices, per_device(): lax.ppermute(row, 'hst', moves(d, 0))  2.87 us
    all_to_all x1, waiting for transfers between devices, per_device(): hidden = lax.all_to_all(hidden, 'tensor', 0, 0)  2.56 us
  transfers between devices with their start and end apart: 10, of which 3 were waited for; matrix products, arithmetic and copies ran while one was open for 2% of the time, Pallas kernels for 43%

profile of v5, /device:TPU:17, one launch (start us, length us, event | category | flops | bytes accessed | tf_op | source)
XLA Modules:
  0.0 111.5 jit_solution(18418997350374393955)
XLA Ops:
  0.0 1.7 %repeat.1 = bf16[8,4,8192]{2,1,0:T(4,128)(2,1)} custom-call(bf16[4,8192]{1,0:T(4,128)(2,1)} %rows_hbm.1), custom_call_target="tpu_custom_call" | custom-call | bytes 1048576 | tf_op jit(solution)/shard_map/gather_hidden/repeat/pallas_call | solution.py:268
  1.7 8.2 %all-to-all-start = ((bf16[8,4,8192]{2,1,0:T(4,128)(2,1)}), bf16[8,4,8192]{2,1,0:T(4,128)(2,1)S(1)}, u32[]{:S(2)}, u32[]{:S(2)}) async-start(bf16[8,4,8192]{2,1,0:T(4,128)(2,1)} %repeat.1), calls=%async_computation | async-start | bytes 1048576 | tf_op jit(solution)/shard_map/gather_hidden/all_to_all | solution.py:328
  9.9 1.8 %select.1 = bf16[64,256]{1,0:T(8,128)(2,1)} custom-call(s32[1,64]{1,0:T(1,128)} %bitcast.12, bf16[512,256]{1,0:T(8,128)(2,1)} %kv_ref.1), custom_call_target="tpu_custom_call" | custom-call | flops 16777216 | bytes 262144 | tf_op jit(solution)/shard_map/select_kept/select/pallas_call | solution.py:268
  11.7 2.6 %collective-permute-start.2 = (bf16[64,256]{1,0:T(8,128)(2,1)}, bf16[64,256]{1,0:T(8,128)(2,1)S(1)}, u32[]{:S(2)}, u32[]{:S(2)}) collective-permute-start(bf16[64,256]{1,0:T(8,128)(2,1)} %select.1), channel_id=1, source_target_pairs={{0,48},{8,56},{16,0},{24,8},{32,16},{40,24},{48,32},{56,40},{64,11... | collective-permute-start | bytes 98312 | tf_op jit(solution)/shard_map/select_kept/ppermute | solution.py:348
  14.3 0.5 collective-permute-start.1
  14.8 0.6 collective-permute-start
  15.4 1.2 %copy-done = bf16[512,1024]{1,0:T(8,128)(2,1)S(1)} copy-done((bf16[512,1024]{1,0:T(8,128)(2,1)S(1)}, bf16[512,1024]{1,0:T(8,128)(2,1)}, u32[]{:S(2)}) %copy-start) | copy-done | bytes 1048600
  16.6 0.9 copy-done.3
  17.6 3.1 %own.2 = (f32[2,7,512]{2,1,0:T(8,128)S(1)}, bf16[7,128,512]{2,1,0:T(8,128)(2,1)S(1)}) custom-call(bf16[512,1024]{1,0:T(8,128)(2,1)S(1)} %copy-done, bf16[512,256]{1,0:T(8,128)(2,1)S(1)} %copy-done.3), custom_call_target="tpu_custom_call" | custom-call | bytes 1024 | tf_op jit(solution)/shard_map/select_kept/own/pallas_call | solution.py:268
  20.6 0.0 copy-start.5
  20.7 0.9 copy-done.5
  21.6 0.0 collective-permute-done
  21.6 0.9 pad_maximum_fusion
  22.5 0.2 collective-permute-start.6
  22.7 2.6 %collective-permute-start.5 = (bf16[4,64,256]{2,1,0:T(8,128)(2,1)S(1)}, bf16[4,64,256]{2,1,0:T(8,128)(2,1)S(1)}, u32[]{:S(2)}, u32[]{:S(2)}) collective-permute-start(bf16[4,64,256]{2,1,0:T(8,128)(2,1)S(1)} %pad_maximum_fusion), channel_id=1, source_target_pairs={{0,128},{8,136},{16,144},{24,152},{32,160},{40,168},{48,176},{56,1... | collective-permute-start | bytes 393224 | tf_op jit(solution)/shard_map/select_kept/ppermute | solution.py:352
  25.3 0.0 collective-permute-start.4
  25.3 2.6 %all-to-all-done.rows_ref = bf16[8,4,8192]{2,1,0:T(4,128)(2,1)S(1)} async-done(((bf16[8,4,8192]{2,1,0:T(4,128)(2,1)}), bf16[8,4,8192]{2,1,0:T(4,128)(2,1)S(1)}, u32[]{:S(2)}, u32[]{:S(2)}) %all-to-all-start) | async-done | bytes 524320 | tf_op jit(solution)/shard_map/gather_hidden/all_to_all | solution.py:328
  27.9 2.2 %copy-done.2 = bf16[8192,256]{1,0:T(8,128)(2,1)S(1)} copy-done((bf16[8192,256]{1,0:T(8,128)(2,1)S(1)}, bf16[8192,256]{1,0:T(8,128)(2,1)}, u32[]{:S(2)}) %copy-start.2) | copy-done | bytes 4194328
  30.1 0.8 project.1
  30.9 0.5 collective-permute-start.3
  31.4 0.8 collective-permute-done.3
  32.2 0.9 broadcast_in_dim.4
  33.1 6.7 %all-to-all-start.1 = ((bf16[16,64,256]{2,1,0:T(8,128)(2,1)}), bf16[16,64,256]{2,1,0:T(8,128)(2,1)S(1)}, u32[]{:S(2)}, u32[]{:S(2)}) async-start(bf16[16,64,256]{2,1,0:T(8,128)(2,1)} %broadcast_in_dim.4), calls=%async_computation.1 | async-start | bytes 1048576 | tf_op jit(solution)/shard_map/project/all_to_all | solution.py:368
  39.8 0.0 collective-permute-done.6
  39.8 0.0 collective-permute-done.5
  39.8 0.0 collective-permute-done.4
  39.9 0.0 copy-start.6
  39.9 1.0 collective-permute-start.7
  40.9 0.8 own.3
  41.7 0.8 collective-permute-done.7.other_ref
  42.5 41.7 %kept.1 = (f32[2,8,512]{2,1,0:T(8,128)S(1)}, bf16[8,128,512]{2,1,0:T(8,128)(2,1)S(1)}) custom-call(s32[1]{0:T(128)} %bitcast.6.at_ref, bf16[512,1024]{1,0:T(8,128)(2,1)S(1)} %copy-done.1, bf16[16,64,256]{2,1,0:T(8,128)(2,1)S(1)} %constant_dynamic-update-slice_fusion.mine_ref, bf16[16,64,256]{2,1,0:T(8,128)(2,1)S(1)} %collective-permute-done.7.other_ref, ...), custom_call_target="tpu_custom_call" | custom-call | flops 4294967296 | bytes 8388608 | tf_op jit(solution)/shard_map/kept/kept/pallas_call | solution.py:268
  84.1 27.2 %anchor.1 = bf16[512,1024]{1,0:T(8,128)(2,1)} custom-call(bf16[512,1024]{1,0:T(8,128)(2,1)S(1)} %copy-done.1, bf16[1024,256]{1,0:T(8,128)(2,1)S(1)} %bitcast.7, f32[2,8,512]{2,1,0:T(8,128)S(1)} %get-tuple-element.55.stat_ref, bf16[8,128,512]{2,1,0:T(8,128)(2,1)S(1)} %get-tuple-element.56.acc_ref), custom_call_target="tpu_custom_call" | custom-call | bytes 1048576 | tf_op jit(solution)/shard_map/anchor/anchor/pallas_call | solution.py:268
  (16 shorter events, 0.1 us)
Async XLA Ops:
  1.7 26.2 %all-to-all-start = ((bf16[8,4,8192]{2,1,0:T(4,128)(2,1)}), bf16[8,4,8192]{2,1,0:T(4,128)(2,1)S(1)}, u32[]{:S(2)}, u32[]{:S(2)}) async-start(bf16[8,4,8192]{2,1,0:T(4,128)(2,1)} %repeat.1), calls=%async_computation | async-start | bytes 1048576 | tf_op jit(solution)/shard_map/gather_hidden/all_to_all | solution.py:328
  11.7 9.9 %collective-permute-start.2 = (bf16[64,256]{1,0:T(8,128)(2,1)}, bf16[64,256]{1,0:T(8,128)(2,1)S(1)}, u32[]{:S(2)}, u32[]{:S(2)}) collective-permute-start(bf16[64,256]{1,0:T(8,128)(2,1)} %select.1), channel_id=1, source_target_pairs={{0,48},{8,56},{16,0},{24,8},{32,16},{40,24},{48,32},{56,40},{64,11... | collective-permute-start | bytes 98312 | tf_op jit(solution)/shard_map/select_kept/ppermute | solution.py:348
  14.3 7.3 %collective-permute-start.1 = (bf16[64,256]{1,0:T(8,128)(2,1)}, bf16[64,256]{1,0:T(8,128)(2,1)S(1)}, u32[]{:S(2)}, u32[]{:S(2)}) collective-permute-start(bf16[64,256]{1,0:T(8,128)(2,1)} %select.1), channel_id=1, source_target_pairs={{0,32},{8,40},{16,48},{24,56},{32,0},{40,8},{48,16},{56,24},{64,96... | collective-permute-start | bytes 98312 | tf_op jit(solution)/shard_map/select_kept/ppermute | solution.py:348
  14.8 6.8 %collective-permute-start = (bf16[64,256]{1,0:T(8,128)(2,1)}, bf16[64,256]{1,0:T(8,128)(2,1)S(1)}, u32[]{:S(2)}, u32[]{:S(2)}) collective-permute-start(bf16[64,256]{1,0:T(8,128)(2,1)} %select.1), channel_id=1, source_target_pairs={{0,16},{8,24},{16,32},{24,40},{32,48},{40,56},{48,0},{56,8},{64,80... | collective-permute-start | bytes 98312 | tf_op jit(solution)/shard_map/select_kept/ppermute | solution.py:348
  15.4 1.2 %copy-start = (bf16[512,1024]{1,0:T(8,128)(2,1)S(1)}, bf16[512,1024]{1,0:T(8,128)(2,1)}, u32[]{:S(2)}) copy-start(bf16[512,1024]{1,0:T(8,128)(2,1)} %q_ref.3) | copy-start | bytes 3145732
  16.6 0.9 copy-start.3
  17.6 23.4 %copy-start.4 = (bf16[512,256]{1,0:T(8,128)(2,1)S(1)}, bf16[512,256]{1,0:T(8,128)(2,1)}, u32[]{:S(2)}) copy-start(bf16[512,256]{1,0:T(8,128)(2,1)} %kv_ref.1) | copy-start | bytes 786436
  20.6 0.9 copy-start.5
  21.6 19.4 %copy-start.1 = (bf16[512,1024]{1,0:T(8,128)(2,1)S(1)}, bf16[512,1024]{1,0:T(8,128)(2,1)}, u32[]{:S(2)}) copy-start(bf16[512,1024]{1,0:T(8,128)(2,1)} %q_ref.3) | copy-start | bytes 3145732
  22.5 17.4 %collective-permute-start.6 = (bf16[4,64,256]{2,1,0:T(8,128)(2,1)S(1)}, bf16[4,64,256]{2,1,0:T(8,128)(2,1)S(1)}, u32[]{:S(2)}, u32[]{:S(2)}) collective-permute-start(bf16[4,64,256]{2,1,0:T(8,128)(2,1)S(1)} %pad_maximum_fusion), channel_id=1, source_target_pairs={{0,192},{8,200},{16,208},{24,216},{32,224},{40,232},{48,240},{56,2... | collective-permute-start | bytes 393224 | tf_op jit(solution)/shard_map/select_kept/ppermute | solution.py:352
  22.7 17.1 %collective-permute-start.5 = (bf16[4,64,256]{2,1,0:T(8,128)(2,1)S(1)}, bf16[4,64,256]{2,1,0:T(8,128)(2,1)S(1)}, u32[]{:S(2)}, u32[]{:S(2)}) collective-permute-start(bf16[4,64,256]{2,1,0:T(8,128)(2,1)S(1)} %pad_maximum_fusion), channel_id=1, source_target_pairs={{0,128},{8,136},{16,144},{24,152},{32,160},{40,168},{48,176},{56,1... | collective-permute-start | bytes 393224 | tf_op jit(solution)/shard_map/select_kept/ppermute | solution.py:352
  25.3 14.5 %collective-permute-start.4 = (bf16[4,64,256]{2,1,0:T(8,128)(2,1)S(1)}, bf16[4,64,256]{2,1,0:T(8,128)(2,1)S(1)}, u32[]{:S(2)}, u32[]{:S(2)}) collective-permute-start(bf16[4,64,256]{2,1,0:T(8,128)(2,1)S(1)} %pad_maximum_fusion), channel_id=1, source_target_pairs={{0,64},{8,72},{16,80},{24,88},{32,96},{40,104},{48,112},{56,120},{... | collective-permute-start | bytes 393224 | tf_op jit(solution)/shard_map/select_kept/ppermute | solution.py:352
  27.9 2.2 %copy-start.2 = (bf16[8192,256]{1,0:T(8,128)(2,1)S(1)}, bf16[8192,256]{1,0:T(8,128)(2,1)}, u32[]{:S(2)}) copy-start(bf16[8192,256]{1,0:T(8,128)(2,1)} %w_ref.1) | copy-start | bytes 12582916
  30.9 1.3 %collective-permute-start.3 = (bf16[32,256]{1,0:T(8,128)(2,1)S(1)}, bf16[32,256]{1,0:T(8,128)(2,1)S(1)}, u32[]{:S(2)}, u32[]{:S(2)}) collective-permute-start(bf16[32,256]{1,0:T(8,128)(2,1)S(1)} %project.1), channel_id=1, source_target_pairs={{0,8},{8,0},{16,24},{24,16},{32,40},{40,32},{48,56},{56,48},{64,72... | collective-permute-start | bytes 49160 | tf_op jit(solution)/shard_map/project/ppermute | solution.py:364
  33.1 51.0 %all-to-all-start.1 = ((bf16[16,64,256]{2,1,0:T(8,128)(2,1)}), bf16[16,64,256]{2,1,0:T(8,128)(2,1)S(1)}, u32[]{:S(2)}, u32[]{:S(2)}) async-start(bf16[16,64,256]{2,1,0:T(8,128)(2,1)} %broadcast_in_dim.4), calls=%async_computation.1 | async-start | bytes 1048576 | tf_op jit(solution)/shard_map/project/all_to_all | solution.py:368
  39.9 2.5 %copy-start.6 = (bf16[7,128,512]{2,1,0:T(8,128)(2,1)S(1)}, bf16[7,128,512]{2,1,0:T(8,128)(2,1)}, u32[]{:S(2)}) copy-start(bf16[7,128,512]{2,1,0:T(8,128)(2,1)} %copy-done.5) | copy-start | bytes 2752516
  39.9 2.5 %collective-permute-start.7 = (bf16[16,64,256]{2,1,0:T(8,128)(2,1)S(1)}, bf16[16,64,256]{2,1,0:T(8,128)(2,1)S(1)}, u32[]{:S(2)}, u32[]{:S(2)}) collective-permute-start(bf16[16,64,256]{2,1,0:T(8,128)(2,1)S(1)} %constant_dynamic-update-slice_fusion.mine_ref), channel_id=1, source_target_pairs={{0,8},{8,0},{16,24},{24,16},{32,40},{40,32},{48,56},{56,48},{64,72... | collective-permute-start | bytes 1572872 | tf_op jit(solution)/shard_map/project/ppermute | solution.py:371
